TPU v7x, 256 devices: a whole 4x4x8 slice. The times are simulated.
256 devices in a mesh: dp: 16 (over y_hi, x, core), seq: 16 (over y_lo, z).
Axes of the slice: x: 4, y: 4 (y_hi: 2, y_lo: 2; y = y_hi * 2 + y_lo), z: 8, core: 2. Of those that a mesh axis runs over, the one named last changes fastest.
Arguments:
- queries: bfloat16 [16, 2048, 2048], P('dp', None, 'seq'), may hold values from -12 to 12
- key_states: bfloat16 [16, 2048, 2048], P('dp', None, 'seq'), may hold values from -12 to 12
- value_states: bfloat16 [16, 2048, 2048], P('dp', None, 'seq'), may hold values from -6 to 6
- grad_payload: bfloat16 [16, 2048, 2048], P('dp', 'seq'), may hold values from -6 to 6
- grad_scale: bfloat16 [16, 2048, 32], P('dp', 'seq'), may hold values from 0.25 to 4
- inputs: bfloat16 [16, 2048, 3072], P('dp', 'seq'), may hold values from -6 to 6
- lengths: int32 [16], P('dp'), may hold values from 1024 to 2048, as said below
Outputs:
- grad_queries: bfloat16 [16, 2048, 2048], P('dp', 'seq')
- grad_keys: bfloat16 [16, 2048, 2048], P('dp', 'seq')
- grad_values: bfloat16 [16, 2048, 2048], P('dp', 'seq')
- weight_grad: float32 [3, 3072, 2048], P(None, 'dp', 'seq')
Inputs may be any that keep to these rules, and one draw needn't show every extreme that they name: `lengths`: padding follows a clip's valid tokens; some clip fills all 2048 tokens.
All inputs are finite; a program needn't handle non-finite values.
Results may differ from a plain program's by a relative error of at most 0.0061.
Values may be sent and summed in bfloat16 or wider, within the bound.
A program may use at most 128 MiB of HBM per device.

v0:
```python
import math

import jax
import jax.numpy as jnp
from jax import lax
from jax.sharding import PartitionSpec as P

HEAD_DIM = 64


def apply_scale(payload, factor, live):
    samples, rows, features = payload.shape
    heads = factor.shape[2]
    scaled = (
        payload.astype(jnp.float32).reshape(samples, rows, heads, features // heads)
        * factor.astype(jnp.float32)[..., None]
    )
    return (scaled * live[:, :, None, None]).reshape(samples, rows, features).astype(jnp.bfloat16)


def clip_backward(query, key_part, value_part, upstream, length):
    positions, heads_here, head_size = query.shape
    factor = head_size ** (-0.5)
    rows = math.gcd(positions, 512)
    usable = jnp.arange(positions) < length

    def advance(index, carry):
        grad_query, key_total, value_total = carry
        start = index * rows
        query_rows = lax.dynamic_slice_in_dim(query, start, rows, 0)
        upstream_rows = lax.dynamic_slice_in_dim(upstream, start, rows, 0)
        scores = (
            jnp.einsum("qhd,khd->hqk", query_rows, key_part, preferred_element_type=jnp.float32)
            * factor
        )
        scores = jnp.where(usable[None, None, :], scores, -1e30)
        highest = jnp.max(scores, axis=2, keepdims=True)
        weights = jnp.exp(scores - highest)
        attention = weights / jnp.sum(weights, axis=2, keepdims=True)
        attention_low = attention.astype(jnp.bfloat16)
        grad_attention = jnp.einsum(
            "qhd,khd->hqk", upstream_rows, value_part, preferred_element_type=jnp.float32
        )
        balance = jnp.sum(attention * grad_attention, axis=2, keepdims=True)
        grad_scores = (attention * (grad_attention - balance) * factor).astype(jnp.bfloat16)
        query_block = jnp.einsum(
            "hqk,khd->qhd", grad_scores, key_part, preferred_element_type=jnp.float32
        ).astype(jnp.bfloat16)
        key_total = key_total + jnp.einsum(
            "hqk,qhd->khd", grad_scores, query_rows, preferred_element_type=jnp.float32
        )
        value_total = value_total + jnp.einsum(
            "hqk,qhd->khd", attention_low, upstream_rows, preferred_element_type=jnp.float32
        )
        grad_query = lax.dynamic_update_slice_in_dim(grad_query, query_block, start, 0)
        return (grad_query, key_total, value_total)

    initial = (
        jnp.zeros_like(query),
        jnp.zeros(query.shape, jnp.float32),
        jnp.zeros(query.shape, jnp.float32),
    )
    grad_query, key_total, value_total = lax.fori_loop(0, positions // rows, advance, initial)
    return (grad_query, key_total.astype(jnp.bfloat16), value_total.astype(jnp.bfloat16))


def shards(queries, key_states, value_states, grad_payload, grad_scale, inputs, lengths):
    samples, positions, width = queries.shape
    heads_here = width // HEAD_DIM
    payload, factor = (
        lax.all_to_all(grad_payload, "seq", split_axis=2, concat_axis=1, tiled=True),
        lax.all_to_all(grad_scale, "seq", split_axis=2, concat_axis=1, tiled=True),
    )
    live = (jnp.arange(positions)[None, :] < lengths[:, None]).astype(jnp.float32)
    upstream = apply_scale(payload, factor, live)
    grad_query, grad_key, grad_value = clip_backward(
        queries[0].reshape(positions, heads_here, HEAD_DIM),
        key_states[0].reshape(positions, heads_here, HEAD_DIM),
        value_states[0].reshape(positions, heads_here, HEAD_DIM),
        upstream[0].reshape(positions, heads_here, HEAD_DIM),
        lengths[0],
    )
    query_list = [grad_query.reshape(positions, width)]
    key_list = [grad_key.reshape(positions, width)]
    value_list = [grad_value.reshape(positions, width)]
    grad_query = jnp.stack(query_list)
    grad_key = jnp.stack(key_list)
    grad_value = jnp.stack(value_list)
    back_query, back_key, back_value = (
        lax.all_to_all(grad_query, "seq", split_axis=1, concat_axis=2, tiled=True),
        lax.all_to_all(grad_key, "seq", split_axis=1, concat_axis=2, tiled=True),
        lax.all_to_all(grad_value, "seq", split_axis=1, concat_axis=2, tiled=True),
    )
    stacked = jnp.stack([grad_query, grad_key, grad_value])
    partial_terms = jnp.einsum(
        "bnd,tbnc->tdc",
        lax.all_gather(inputs, "seq", axis=1, tiled=True),
        stacked,
        preferred_element_type=jnp.float32,
    )
    weight_grad = lax.psum_scatter(partial_terms, "dp", scatter_dimension=1, tiled=True)
    return (back_query, back_key, back_value, weight_grad)


def solution(mesh):
    return jax.shard_map(
        shards,
        mesh=mesh,
        in_specs=(
            P("dp", None, "seq"),
            P("dp", None, "seq"),
            P("dp", None, "seq"),
            P("dp", "seq", None),
            P("dp", "seq", None),
            P("dp", "seq", None),
            P("dp"),
        ),
        out_specs=(
            P("dp", "seq", None),
            P("dp", "seq", None),
            P("dp", "seq", None),
            P(None, "dp", "seq"),
        ),
        check_vma=False,
    )
```

profile of v0, /device:TPU:2, one launch (start us, length us, event | category | flops | bytes accessed | tf_op | source)
XLA Modules:
  0.0 381.2 jit_solution(562811752046237730)
XLA Ops:
  9.2 9.6 %all-to-all-start.1 = ((bf16[16,2,128]{2,1,0:T(2,128)(2,1)}), bf16[16,2,128]{2,1,0:T(2,128)(2,1)S(1)}, u32[]{:S(2)}, u32[]{:S(2)}) async-start(bf16[16,2,128]{2,1,0:T(2,128)(2,1)} %bitcast.82), calls=%async_computation.1 | async-start | bytes 16384 | tf_op jit(solution)/shard_map/all_to_all | solution.py:72
  21.7 11.5 %reduce = bf16[2048,128]{1,0:T(8,128)(2,1)S(1)} reduce(bf16[2048,1,128]{2,1,0:T(2,128)(2,1)S(1)} %bitcast.102, bf16[]{:T(256)} %broadcast.67), dimensions={1}, to_apply=%bitcast.63.reduce_sub_computation | reduce | bytes 1048578
  34.1 8.1 %all-to-all-start = ((bf16[16,2,8192]{2,1,0:T(2,128)(2,1)}), bf16[16,2,8192]{2,1,0:T(2,128)(2,1)S(1)}, u32[]{:S(2)}, u32[]{:S(2)}) async-start(bf16[16,2,8192]{2,1,0:T(2,128)(2,1)} %reshape.81), calls=%async_computation | async-start | bytes 1048576 | tf_op jit(solution)/shard_map/all_to_all | solution.py:71
  46.6 18.1 %all-to-all-done = bf16[16,2,8192]{2,1,0:T(2,128)(2,1)S(1)} async-done(((bf16[16,2,8192]{2,1,0:T(2,128)(2,1)}), bf16[16,2,8192]{2,1,0:T(2,128)(2,1)S(1)}, u32[]{:S(2)}, u32[]{:S(2)}) %all-to-all-start) | async-done | bytes 524320 | tf_op jit(solution)/shard_map/all_to_all | solution.py:71
  67.6 186.6 %while.18 = (s32[]{:T(128)}, bf16[2048,2,64]{0,2,1:T(8,128)(2,1)S(1)}, f32[2048,2,64]{0,2,1:T(8,128)}, f32[2048,2,64]{0,2,1:T(8,128)}, bf16[2048,2,64]{0,2,1:T(8...) while((s32[]{:T(128)}, ...), condition=%wide.region_4.5_spmd.clone, body=%wide.region_0.4_spmd.clone.sunk | while | flops 1385244672 | bytes 107114752 | solution.py:63
  68.2 7.0 %fusion.112 = (f32[2,512]{1,0:T(2,128)S(1)}, f32[2,512,2048]{2,1,0:T(8,128)}) fusion(pred[2048]{0:T(1024)(128)(4,1)S(1)} %iota_compare_fusion.3, bf16[2048,2,64]{0,2,1:T(8,128)(2,1)} %get-tuple-element.322, bf16[2048,2,64]{0,2,1:T(8,128)(2,1)S(1)} %get-tuple-element.321, s32[]{:T(128)S(6)} %select_n.32), kind=kOutput, calls=%fused_computation.57.clone.1 | convolution fusion | flops 276826112 | bytes 9050116 | tf_op jit(solution)/shard_map/while/body/eval_jaxpr/sub | solution.py:38
  79.7 15.7 %fusion.114 = f32[2048,2,64]{0,2,1:T(8,128)S(1)} fusion(f32[2,512,2048]{2,1,0:T(8,128)} %fusion.111, f32[2048,2,64]{0,2,1:T(8,128)S(1)} %copy-done, pred[]{:T(512)S(6)} %compare.3, bf16[2048,2,64]{0,2,1:T(8,128)(2,1)S(1)} %get-tuple-element.321, s32[]{:T(128)S(6)} %select_n.32, f32[2,512,2048]{2,1,0:T(8,128)} %get-tuple-element.289, ...), kind=kOutput, calls=%fused_computation.20.clone.1 | convolution fusion | flops 283642880 | bytes 35790852 | tf_op jit(solution)/shard_map/while/body/eval_jaxpr/hqk,qhd->khd/dot_general | solution.py:49
  101.2 13.0 %fusion.113 = bf16[2048,2,64]{0,2,1:T(8,128)(2,1)S(1)} fusion(bf16[2048,2,64]{0,2,1:T(8,128)(2,1)S(1)} %get-tuple-element.305, s32[]{:T(128)S(6)} %select_n.32, bf16[2048,2,64]{0,2,1:T(8,128)(2,1)} %get-tuple-element.322, f32[2,512,2048]{2,1,0:T(8,128)} %fusion.111, f32[2,512,2048]{2,1,0:T(8,128)} %get-tuple-element.289, ...), kind=kOutput, calls=%fused_computation.23.clone.1 | convolution fusion | flops 283184128 | bytes 34217988 | tf_op jit(solution)/shard_map/while/body/eval_jaxpr/hqk,khd->qhd/dot_general | solution.py:46
  114.9 7.0 %fusion.112 = (f32[2,512]{1,0:T(2,128)S(1)}, f32[2,512,2048]{2,1,0:T(8,128)}) fusion(pred[2048]{0:T(1024)(128)(4,1)S(1)} %iota_compare_fusion.3, bf16[2048,2,64]{0,2,1:T(8,128)(2,1)} %get-tuple-element.322, bf16[2048,2,64]{0,2,1:T(8,128)(2,1)S(1)} %get-tuple-element.321, s32[]{:T(128)S(6)} %select_n.32), kind=kOutput, calls=%fused_computation.57.clone.1 | convolution fusion | flops 276826112 | bytes 9050116 | tf_op jit(solution)/shard_map/while/body/eval_jaxpr/sub | solution.py:38
  126.4 15.7 %fusion.114 = f32[2048,2,64]{0,2,1:T(8,128)S(1)} fusion(f32[2,512,2048]{2,1,0:T(8,128)} %fusion.111, f32[2048,2,64]{0,2,1:T(8,128)S(1)} %copy-done, pred[]{:T(512)S(6)} %compare.3, bf16[2048,2,64]{0,2,1:T(8,128)(2,1)S(1)} %get-tuple-element.321, s32[]{:T(128)S(6)} %select_n.32, f32[2,512,2048]{2,1,0:T(8,128)} %get-tuple-element.289, ...), kind=kOutput, calls=%fused_computation.20.clone.1 | convolution fusion | flops 283642880 | bytes 35790852 | tf_op jit(solution)/shard_map/while/body/eval_jaxpr/hqk,qhd->khd/dot_general | solution.py:49
  148.1 13.0 %fusion.113 = bf16[2048,2,64]{0,2,1:T(8,128)(2,1)S(1)} fusion(bf16[2048,2,64]{0,2,1:T(8,128)(2,1)S(1)} %get-tuple-element.305, s32[]{:T(128)S(6)} %select_n.32, bf16[2048,2,64]{0,2,1:T(8,128)(2,1)} %get-tuple-element.322, f32[2,512,2048]{2,1,0:T(8,128)} %fusion.111, f32[2,512,2048]{2,1,0:T(8,128)} %get-tuple-element.289, ...), kind=kOutput, calls=%fused_computation.23.clone.1 | convolution fusion | flops 283184128 | bytes 34217988 | tf_op jit(solution)/shard_map/while/body/eval_jaxpr/hqk,khd->qhd/dot_general | solution.py:46
  173.3 15.7 %fusion.114 = f32[2048,2,64]{0,2,1:T(8,128)S(1)} fusion(f32[2,512,2048]{2,1,0:T(8,128)} %fusion.111, f32[2048,2,64]{0,2,1:T(8,128)S(1)} %copy-done, pred[]{:T(512)S(6)} %compare.3, bf16[2048,2,64]{0,2,1:T(8,128)(2,1)S(1)} %get-tuple-element.321, s32[]{:T(128)S(6)} %select_n.32, f32[2,512,2048]{2,1,0:T(8,128)} %get-tuple-element.289, ...), kind=kOutput, calls=%fused_computation.20.clone.1 | convolution fusion | flops 283642880 | bytes 35790852 | tf_op jit(solution)/shard_map/while/body/eval_jaxpr/hqk,qhd->khd/dot_general | solution.py:49
  194.9 12.7 %fusion.113 = bf16[2048,2,64]{0,2,1:T(8,128)(2,1)S(1)} fusion(bf16[2048,2,64]{0,2,1:T(8,128)(2,1)S(1)} %get-tuple-element.305, s32[]{:T(128)S(6)} %select_n.32, bf16[2048,2,64]{0,2,1:T(8,128)(2,1)} %get-tuple-element.322, f32[2,512,2048]{2,1,0:T(8,128)} %fusion.111, f32[2,512,2048]{2,1,0:T(8,128)} %get-tuple-element.289, ...), kind=kOutput, calls=%fused_computation.23.clone.1 | convolution fusion | flops 283184128 | bytes 34217988 | tf_op jit(solution)/shard_map/while/body/eval_jaxpr/hqk,khd->qhd/dot_general | solution.py:46
  219.8 15.7 %fusion.114 = f32[2048,2,64]{0,2,1:T(8,128)S(1)} fusion(f32[2,512,2048]{2,1,0:T(8,128)} %fusion.111, f32[2048,2,64]{0,2,1:T(8,128)S(1)} %copy-done, pred[]{:T(512)S(6)} %compare.3, bf16[2048,2,64]{0,2,1:T(8,128)(2,1)S(1)} %get-tuple-element.321, s32[]{:T(128)S(6)} %select_n.32, f32[2,512,2048]{2,1,0:T(8,128)} %get-tuple-element.289, ...), kind=kOutput, calls=%fused_computation.20.clone.1 | convolution fusion | flops 283642880 | bytes 35790852 | tf_op jit(solution)/shard_map/while/body/eval_jaxpr/hqk,qhd->khd/dot_general | solution.py:49
  241.4 12.7 %fusion.113 = bf16[2048,2,64]{0,2,1:T(8,128)(2,1)S(1)} fusion(bf16[2048,2,64]{0,2,1:T(8,128)(2,1)S(1)} %get-tuple-element.305, s32[]{:T(128)S(6)} %select_n.32, bf16[2048,2,64]{0,2,1:T(8,128)(2,1)} %get-tuple-element.322, f32[2,512,2048]{2,1,0:T(8,128)} %fusion.111, f32[2,512,2048]{2,1,0:T(8,128)} %get-tuple-element.289, ...), kind=kOutput, calls=%fused_computation.23.clone.1 | convolution fusion | flops 283184128 | bytes 34217988 | tf_op jit(solution)/shard_map/while/body/eval_jaxpr/hqk,khd->qhd/dot_general | solution.py:46
  256.8 10.1 %fusion.68 = f32[3,3072,128]{1,2,0:T(8,128)} fusion(bf16[1,2048,3072]{2,1,0:T(8,128)(2,1)} %all-gather.2.cloned.1.call-done, bf16[1,1,2048,128]{2,3,0,1:T(8,128)(2,1)S(1)} %bitcast.107, bf16[1,1,2048,128]{2,3,0,1:T(8,128)(2,1)S(1)} %bitcast.109, bf16[1,1,2048,128]{2,3,0,1:T(8,128)(2,1)S(1)} %bitcast.111), kind=kOutput, calls=%fused_computation.47 | convolution fusion | flops 4833411072 | bytes 18874368 | tf_op jit(solution)/shard_map/bnd,tbnc->tdc/dot_general | solution.py:95
  266.9 7.0 %copy.54 = f32[3,3072,128]{2,0,1:T(4,128)} copy(f32[3,3072,128]{1,2,0:T(8,128)} %fusion.68) | data formatting | bytes 9437184
  280.3 12.0 %reduce.2 = bf16[2048,128]{1,0:T(8,128)(2,1)S(1)} reduce(bf16[2048,1,128]{2,1,0:T(2,128)(2,1)S(1)} %bitcast.105, bf16[]{:T(256)} %broadcast.67), dimensions={1}, to_apply=%bitcast.69.reduce_sub_computation | reduce | bytes 1048578
  297.6 11.5 %reduce.3 = bf16[2048,128]{1,0:T(8,128)(2,1)S(1)} reduce(bf16[2048,1,128]{2,1,0:T(2,128)(2,1)S(1)} %bitcast.106, bf16[]{:T(256)} %broadcast.67), dimensions={1}, to_apply=%bitcast.71.reduce_sub_computation | reduce | bytes 1048578
  311.0 7.4 %all-to-all-start.4 = ((bf16[16,2,8192]{2,1,0:T(2,128)(2,1)}), bf16[16,2,8192]{2,1,0:T(2,128)(2,1)S(1)}, u32[]{:S(2)}, u32[]{:S(2)}) async-start(bf16[16,2,8192]{2,1,0:T(2,128)(2,1)} %reshape.89), calls=%async_computation.4 | async-start | bytes 1048576 | tf_op jit(solution)/shard_map/all_to_all | solution.py:92
  319.2 11.5 %reduce.1 = bf16[2048,128]{1,0:T(8,128)(2,1)S(1)} reduce(bf16[2048,1,128]{2,1,0:T(2,128)(2,1)S(1)} %bitcast.103, bf16[]{:T(256)} %broadcast.67), dimensions={1}, to_apply=%bitcast.67.reduce_sub_computation | reduce | bytes 1048578
  332.0 7.9 %all-to-all-start.2 = ((bf16[16,2,8192]{2,1,0:T(2,128)(2,1)}), bf16[16,2,8192]{2,1,0:T(2,128)(2,1)S(1)}, u32[]{:S(2)}, u32[]{:S(2)}) async-start(bf16[16,2,8192]{2,1,0:T(2,128)(2,1)} %reshape.85), calls=%async_computation.2 | async-start | bytes 1048576 | tf_op jit(solution)/shard_map/all_to_all | solution.py:90
  343.7 9.6 %all-to-all-done.2 = bf16[16,2,8192]{2,1,0:T(2,128)(2,1)S(1)} async-done(((bf16[16,2,8192]{2,1,0:T(2,128)(2,1)}), bf16[16,2,8192]{2,1,0:T(2,128)(2,1)S(1)}, u32[]{:S(2)}, u32[]{:S(2)}) %all-to-all-start.2) | async-done | bytes 524320 | tf_op jit(solution)/shard_map/all_to_all | solution.py:90
  355.2 17.2 %reduce-scatter.4.cloned.1.call-done = f32[192,384]{1,0:T(8,128)} async-done(((f32[3072,384]{1,0:T(8,128)}), f32[192,384]{1,0:T(8,128)}) %reduce-scatter.4.cloned.1.call-update) | async-done | bytes 294928
  (83 shorter events, 96.0 us)
Async XLA Ops:
  7.2 39.1 %copy-start.2 = (bf16[1,2048,128]{2,1,0:T(8,128)(2,1)S(1)}, bf16[1,2048,128]{2,1,0:T(8,128)(2,1)}, u32[]{:S(2)}) copy-start(bf16[1,2048,128]{2,1,0:T(8,128)(2,1)} %param.11) | copy-start | bytes 1572868
  7.2 249.6 %all-gather.2.cloned.1.call-start = ((), (), s32[]{:S(2)}) async-start(), calls=%async_computation.6 | async-start | bytes 13369344 | tf_op jit(solution)/shard_map/all_gather | solution.py:97
  9.2 24.9 %all-to-all-start.1 = ((bf16[16,2,128]{2,1,0:T(2,128)(2,1)}), bf16[16,2,128]{2,1,0:T(2,128)(2,1)S(1)}, u32[]{:S(2)}, u32[]{:S(2)}) async-start(bf16[16,2,128]{2,1,0:T(2,128)(2,1)} %bitcast.82), calls=%async_computation.1 | async-start | bytes 16384 | tf_op jit(solution)/shard_map/all_to_all | solution.py:72
  34.1 30.6 %all-to-all-start = ((bf16[16,2,8192]{2,1,0:T(2,128)(2,1)}), bf16[16,2,8192]{2,1,0:T(2,128)(2,1)S(1)}, u32[]{:S(2)}, u32[]{:S(2)}) async-start(bf16[16,2,8192]{2,1,0:T(2,128)(2,1)} %reshape.81), calls=%async_computation | async-start | bytes 1048576 | tf_op jit(solution)/shard_map/all_to_all | solution.py:71
  42.3 330.1 %reduce-scatter.4.cloned.1.call-start = ((), (), s32[]{:S(2)}) async-start(), calls=%async_computation.7 | async-start | bytes 5013504
  68.2 11.5 %copy-start = (f32[2048,2,64]{0,2,1:T(8,128)S(1)}, f32[2048,2,64]{0,2,1:T(8,128)}, u32[]{:S(2)}) copy-start(f32[2048,2,64]{0,2,1:T(8,128)} %get-tuple-element.306) | copy-start | bytes 3145732 | tf_op jit(solution)/shard_map/while
  95.4 18.8 %copy-start.1 = (f32[2048,2,64]{0,2,1:T(8,128)}, f32[2048,2,64]{0,2,1:T(8,128)S(1)}, u32[]{:S(2)}) copy-start(f32[2048,2,64]{0,2,1:T(8,128)S(1)} %fusion.114) | copy-start | bytes 3145732 | tf_op jit(solution)/shard_map/while
  114.9 11.5 %copy-start = (f32[2048,2,64]{0,2,1:T(8,128)S(1)}, f32[2048,2,64]{0,2,1:T(8,128)}, u32[]{:S(2)}) copy-start(f32[2048,2,64]{0,2,1:T(8,128)} %get-tuple-element.306) | copy-start | bytes 3145732 | tf_op jit(solution)/shard_map/while
  142.1 19.1 %copy-start.1 = (f32[2048,2,64]{0,2,1:T(8,128)}, f32[2048,2,64]{0,2,1:T(8,128)S(1)}, u32[]{:S(2)}) copy-start(f32[2048,2,64]{0,2,1:T(8,128)S(1)} %fusion.114) | copy-start | bytes 3145732 | tf_op jit(solution)/shard_map/while
  161.8 11.5 %copy-start = (f32[2048,2,64]{0,2,1:T(8,128)S(1)}, f32[2048,2,64]{0,2,1:T(8,128)}, u32[]{:S(2)}) copy-start(f32[2048,2,64]{0,2,1:T(8,128)} %get-tuple-element.306) | copy-start | bytes 3145732 | tf_op jit(solution)/shard_map/while
  189.0 18.7 %copy-start.1 = (f32[2048,2,64]{0,2,1:T(8,128)}, f32[2048,2,64]{0,2,1:T(8,128)S(1)}, u32[]{:S(2)}) copy-start(f32[2048,2,64]{0,2,1:T(8,128)S(1)} %fusion.114) | copy-start | bytes 3145732 | tf_op jit(solution)/shard_map/while
  208.3 11.5 %copy-start = (f32[2048,2,64]{0,2,1:T(8,128)S(1)}, f32[2048,2,64]{0,2,1:T(8,128)}, u32[]{:S(2)}) copy-start(f32[2048,2,64]{0,2,1:T(8,128)} %get-tuple-element.306) | copy-start | bytes 3145732 | tf_op jit(solution)/shard_map/while
  235.5 18.7 %copy-start.1 = (f32[2048,2,64]{0,2,1:T(8,128)}, f32[2048,2,64]{0,2,1:T(8,128)S(1)}, u32[]{:S(2)}) copy-start(f32[2048,2,64]{0,2,1:T(8,128)S(1)} %fusion.114) | copy-start | bytes 3145732 | tf_op jit(solution)/shard_map/while
  293.2 17.8 %all-to-all-start.3 = ((bf16[16,2,8192]{2,1,0:T(2,128)(2,1)}), bf16[16,2,8192]{2,1,0:T(2,128)(2,1)S(1)}, u32[]{:S(2)}, u32[]{:S(2)}) async-start(bf16[16,2,8192]{2,1,0:T(2,128)(2,1)} %reshape.87), calls=%async_computation.3 | async-start | bytes 1048576 | tf_op jit(solution)/shard_map/all_to_all | solution.py:91
  311.0 20.9 %all-to-all-start.4 = ((bf16[16,2,8192]{2,1,0:T(2,128)(2,1)}), bf16[16,2,8192]{2,1,0:T(2,128)(2,1)S(1)}, u32[]{:S(2)}, u32[]{:S(2)}) async-start(bf16[16,2,8192]{2,1,0:T(2,128)(2,1)} %reshape.89), calls=%async_computation.4 | async-start | bytes 1048576 | tf_op jit(solution)/shard_map/all_to_all | solution.py:92
  332.0 21.3 %all-to-all-start.2 = ((bf16[16,2,8192]{2,1,0:T(2,128)(2,1)}), bf16[16,2,8192]{2,1,0:T(2,128)(2,1)S(1)}, u32[]{:S(2)}, u32[]{:S(2)}) async-start(bf16[16,2,8192]{2,1,0:T(2,128)(2,1)} %reshape.85), calls=%async_computation.2 | async-start | bytes 1048576 | tf_op jit(solution)/shard_map/all_to_all | solution.py:90
Sparse Core Ops, SparseCore 0:
  9.8 157.3 all-gather.1
  279.6 92.7 reduce-scatter.3
where the time goes:
time: 387 us; the launch traced here: 381 us
  matrix products  194 us (50%)
  other arithmetic  53 us (14%)
  waiting for transfers between devices  47 us (12%)
  starting transfers between devices  36.7 us (9%)
  local copies, waits for them, and re-layouts  35.3 us (9%)
  between operations  15.2 us (4%)
    dot_general x4, matrix products, advance(): jnp.einsum('hqk,qhd->khd', grad_scores, query_rows, preferred_element_typ...  62.6 us
    dot_general x4, matrix products, advance(): jnp.einsum('hqk,khd->qhd', grad_scores, key_part, preferred_element_type=...  51.5 us
    unnamed x6, other arithmetic  46.6 us
    unnamed x28, local copies, waits for them, and re-layouts  31.3 us
    sub x4, matrix products, advance(): weights = jnp.exp(scores - highest)  27.9 us
    dot_general x4, matrix products, advance(): jnp.einsum('hqk,qhd->khd', attention_low, upstream_rows, preferred_elemen...  23.7 us
    all_to_all x1, waiting for transfers between devices, shards(): lax.all_to_all(grad_payload, 'seq', split_axis=2, concat_axis=1, tiled=True)  18.1 us
    dot_general x4, matrix products, advance(): jnp.einsum('qhd,khd->hqk', upstream_rows, value_part, preferred_element_t...  17.9 us
  transfers between devices with their start and end apart: 7, of which 5 were waited for; matrix products, arithmetic and copies ran while one was open for 68% of the time, Pallas kernels for 0%

commit v1 on v0

v1 whole, which is shorter than its diff:
```python
import jax
import jax.numpy as jnp
from jax import lax
from jax.experimental import pallas as pl
from jax.experimental.pallas import tpu as pltpu
from jax.sharding import PartitionSpec as P

HEAD_DIM = 64
LANES = 128
ROWS = 512
KEYS = 256
f32 = jnp.float32
bf16 = jnp.bfloat16


def dot(a, b, over=((1,), (0,))):
    return lax.dot_general(a, b, (over, ((), ())), preferred_element_type=f32)


def attention_kernel(
    length_ref, q_ref, k_ref, v_ref, u_ref, dq_ref, dk_ref, dv_ref,
    keys, keys_t, scores, weights, grads, key_total, value_total,
):
    positions = q_ref.shape[0]
    chunks = [slice(at, at + KEYS) for at in range(0, positions, KEYS)]
    length = length_ref[0]
    position = lax.broadcasted_iota(jnp.int32, (positions, LANES), 0)
    lane = lax.broadcasted_iota(jnp.int32, (positions, LANES), 1)
    keys[:, :LANES] = k_ref[...]
    keys[:, LANES:] = jnp.where((lane == 0) & (position >= length), -1e30, 0.0).astype(bf16)
    keys_t[...] = k_ref[...].T
    key_total[...] = jnp.zeros_like(key_total)
    value_total[...] = jnp.zeros_like(value_total)
    lane_row = lax.broadcasted_iota(jnp.int32, (ROWS, LANES), 1)
    ones = jnp.where(lane_row == 0, 1.0, 0.0).astype(bf16)

    def block(index, _):
        start = pl.multiple_of(index * ROWS, ROWS)
        query = q_ref[pl.ds(start, ROWS), :].astype(f32) * HEAD_DIM**-0.5
        upstream = u_ref[pl.ds(start, ROWS), :].astype(f32)
        parts = []
        for head in range(LANES // HEAD_DIM):
            mine = lane_row // HEAD_DIM == head
            q = jnp.where(mine, query, 0.0).astype(bf16)
            u = jnp.where(mine, upstream, 0.0).astype(bf16)
            q_ones = jnp.concatenate([q, ones], axis=1)
            top = jnp.full((8, ROWS), -3e38, f32)
            for chunk in chunks:
                s = dot(keys[chunk, :], q_ones, ((1,), (1,)))
                scores[chunk, :] = s
                top = jnp.maximum(top, jnp.max(s.reshape(KEYS // 8, 8, ROWS), axis=0))
            top = jnp.max(top, axis=0, keepdims=True)
            mass = jnp.zeros((8, ROWS), f32)
            balance = jnp.zeros((8, ROWS), f32)
            for chunk in chunks:
                e = jnp.exp(scores[chunk, :] - top)
                weights[chunk, :] = e
                g = dot(v_ref[chunk, :], u, ((1,), (1,)))
                grads[chunk, :] = g
                mass += jnp.sum(e.reshape(KEYS // 8, 8, ROWS), axis=0)
                balance += jnp.sum((e * g).reshape(KEYS // 8, 8, ROWS), axis=0)
            scale = 1.0 / jnp.sum(mass, axis=0, keepdims=True)
            balance = jnp.sum(balance, axis=0, keepdims=True) * scale
            grad_q = jnp.zeros((HEAD_DIM, ROWS), f32)
            for chunk in chunks:
                p = weights[chunk, :] * scale
                ds = (p * (grads[chunk, :] - balance)).astype(bf16)
                value_total[chunk, :] += dot(p.astype(bf16), u)
                key_total[chunk, :] += dot(ds, q)
                grad_q += dot(keys_t[head * HEAD_DIM : (head + 1) * HEAD_DIM, chunk], ds)
            parts.append(grad_q * HEAD_DIM**-0.5)
        dq_ref[pl.ds(start, ROWS), :] = jnp.concatenate(parts, axis=0).T.astype(bf16)
        return 0

    lax.fori_loop(0, positions // ROWS, block, 0)
    dk_ref[...] = key_total[...].astype(bf16)
    dv_ref[...] = value_total[...].astype(bf16)


def attention_backward(length, q, k, v, u):
    positions = q.shape[0]
    whole = pl.BlockSpec(memory_space=pltpu.VMEM)
    return pl.pallas_call(
        attention_kernel,
        out_shape=[jax.ShapeDtypeStruct(q.shape, bf16)] * 3,
        in_specs=[pl.BlockSpec(memory_space=pltpu.SMEM)] + [whole] * 4,
        out_specs=[whole] * 3,
        scratch_shapes=[
            pltpu.VMEM((positions, 2 * LANES), bf16),
            pltpu.VMEM((LANES, positions), bf16),
            pltpu.VMEM((positions, ROWS), f32),
            pltpu.VMEM((positions, ROWS), f32),
            pltpu.VMEM((positions, ROWS), f32),
            pltpu.VMEM((positions, LANES), f32),
            pltpu.VMEM((positions, LANES), f32),
        ],
        compiler_params=pltpu.CompilerParams(vmem_limit_bytes=48 * 2**20),
        name="attention",
    )(length, q, k, v, u)


def shards(queries, key_states, value_states, grad_payload, grad_scale, inputs, lengths):
    _, positions, width = queries.shape
    _, rows, features = grad_payload.shape
    heads = grad_scale.shape[2]
    owners = features // width
    tokens = lax.axis_index("seq") * rows + jnp.arange(rows)
    live = (tokens < lengths[0]).astype(f32)
    scaled = grad_payload[0].astype(f32).reshape(rows, heads, HEAD_DIM) * grad_scale[0].astype(f32)[..., None]
    upstream = (scaled * live[:, None, None]).astype(bf16).reshape(rows, owners, width)
    upstream = lax.all_to_all(upstream.transpose(1, 0, 2), "seq", split_axis=0, concat_axis=0)
    grads = attention_backward(
        lengths, queries[0], key_states[0], value_states[0], upstream.reshape(positions, width)
    )
    gathered = lax.all_gather(inputs[0], "seq", axis=0, tiled=True)
    terms = jnp.stack([dot(gathered, grad, ((0,), (0,))) for grad in grads])
    weight_grad = lax.psum_scatter(terms, "dp", scatter_dimension=1, tiled=True)
    back = []
    for grad in grads:
        blocks = lax.all_to_all(grad.reshape(owners, rows, width), "seq", split_axis=0, concat_axis=0)
        back.append(blocks.transpose(1, 0, 2).reshape(1, rows, features))
    return (*back, weight_grad)


def solution(mesh):
    return jax.shard_map(
        shards,
        mesh=mesh,
        in_specs=(
            P("dp", None, "seq"),
            P("dp", None, "seq"),
            P("dp", None, "seq"),
            P("dp", "seq", None),
            P("dp", "seq", None),
            P("dp", "seq", None),
            P("dp"),
        ),
        out_specs=(
            P("dp", "seq", None),
            P("dp", "seq", None),
            P("dp", "seq", None),
            P(None, "dp", "seq"),
        ),
        check_vma=False,
    )
```

time: 387 us -> 293 us (0.76); the launches traced: 381 us -> 293 us
  matrix products: 194 us -> 10.3 us
  waiting for transfers between devices: 47 us -> 136 us
  blocking collectives: 0 us -> 70.6 us
  other arithmetic: 53 us -> 3.62 us
  starting transfers between devices: 36.7 us -> 4.64 us
  Pallas kernels: 0 us -> 31.2 us
  local copies, waits for them, and re-layouts: 35.3 us -> 21.7 us
    dot_general x17 -> x3, matrix products: 166 us -> 10.3 us  [dot(): return lax.dot_general(a, b, (over, ((), ())), preferred_element_type=f32)]
    all_gather x1, waiting for transfers between devices: 0.02 us -> 90.5 us  [shards(): gathered = lax.all_gather(inputs[0], 'seq', axis=0, tiled=True)]
    all_to_all x0 -> x3, blocking collectives: none -> 70.6 us  [the longest x2 40.4 us: shards(): lax.all_to_all(grad.reshape(owners, rows, width), 'seq', split_axis=0, co...]
    unnamed x6 -> x0, other arithmetic: 46.6 us -> none
    all_to_all x5 -> x1, starting transfers between devices: 36.6 us -> 4.56 us  [shards(): lax.all_to_all(grad.reshape(owners, rows, width), 'seq', split_axis=0, co...]
    pallas_call x0 -> x1, Pallas kernels: none -> 31.2 us  [attention_backward(): pl.pallas_call(attention_kernel, out_shape=[jax.ShapeDtypeStruct(q.shape,...]
    sub x4 -> x0, matrix products: 27.9 us -> none  [advance(): weights = jnp.exp(scores - highest)]
    all_to_all x5 -> x1, waiting for transfers between devices: 29 us -> 11.8 us  [shards(): lax.all_to_all(grad.reshape(owners, rows, width), 'seq', split_axis=0, co...]
  transfers between devices with their start and end apart: 7 -> 3, of which waited for: 5 -> 3; matrix products, arithmetic and copies ran while one was open for 68% -> 2% of each run, Pallas kernels for 0% -> 11%
where the time goes in v1:
time: 293 us
  waiting for transfers between devices  136 us (46%)
  blocking collectives  70.6 us (24%)
  Pallas kernels  31.2 us (11%)
  local copies, waits for them, and re-layouts  21.7 us (7%)
  between operations  14.8 us (5%)
  matrix products  10.3 us (4%)
  starting transfers between devices  4.64 us (2%)
  other arithmetic  3.62 us (1%)
    all_gather x1, waiting for transfers between devices, shards(): gathered = lax.all_gather(inputs[0], 'seq', axis=0, tiled=True)  90.5 us
    all_to_all x2, blocking collectives, shards(): lax.all_to_all(grad.reshape(owners, rows, width), 'seq', split_axis=0, co...  40.4 us
    unnamed x3, waiting for transfers between devices  33.6 us
    pallas_call x1, Pallas kernels, attention_backward(): pl.pallas_call(attention_kernel, out_shape=[jax.ShapeDtypeStruct(q.shape,...  31.2 us
    all_to_all x1, blocking collectives, shards(): lax.all_to_all(upstream.transpose(1, 0, 2), 'seq', split_axis=0, concat_a...  30.3 us
    unnamed x12, local copies, waits for them, and re-layouts  16 us
    all_to_all x1, waiting for transfers between devices, shards(): lax.all_to_all(grad.reshape(owners, rows, width), 'seq', split_axis=0, co...  11.8 us
    dot_general x3, matrix products, dot(): return lax.dot_general(a, b, (over, ((), ())), preferred_element_type=f32)  10.3 us
  transfers between devices with their start and end apart: 3, of which 3 were waited for; matrix products, arithmetic and copies ran while one was open for 2% of the time, Pallas kernels for 11%

profile of v1, /device:TPU:2, one launch (start us, length us, event | category | flops | bytes accessed | tf_op | source)
XLA Modules:
  0.0 292.8 jit_solution(11218449632248053085)
XLA Ops:
  7.2 0.7 all-gather.3.cloned.1.call-update
  8.6 1.2 copy.23
  9.9 0.7 bitcast_convert_fusion
  10.8 30.3 %all_to_all.20 = bf16[16,128,128]{1,2,0:T(8,128)(2,1)S(1)} all-to-all(bf16[16,128,128]{1,2,0:T(8,128)(2,1)S(1)} %fusion.17), channel_id=1, replica_groups=mesh['dp'=16,'seq'=16] {'seq'}, dimensions={0} | all-to-all | bytes 1048576 | tf_op jit(solution)/shard_map/all_to_all | solution.py:111
  41.4 31.2 %attention.1 = (bf16[2048,128]{1,0:T(8,128)(2,1)S(1)}, bf16[2048,128]{1,0:T(8,128)(2,1)S(1)}, bf16[2048,128]{1,0:T(8,128)(2,1)}) custom-call(s32[1]{0:T(128)} %copy.35.length_ref, bf16[2048,128]{1,0:T(8,128)(2,1)S(1)} %bitcast.65, bf16[2048,128]{1,0:T(8,128)(2,1)S(1)} %bitcast.66, bf16[2048,128]{1,0:T(8,128)(2,1)S(1)} %bitcast.67, bf16[2048,128]{1,0:T(8,128)(2,1)S(1)} %bitcast.64), custom_call_target="tpu_custom_call" | custom-call | tf_op jit(solution)/shard_map/attention/pallas_call | solution.py:83
  72.6 90.5 %all-gather.3.cloned.1.call-done = bf16[1,2048,3072]{2,1,0:T(8,128)(2,1)} async-done(((bf16[1,128,3072]{2,1,0:T(8,128)(2,1)}), bf16[1,2048,3072]{2,1,0:T(8,128)(2,1)}) %all-gather.3.cloned.1.call-update) | async-done | bytes 12582928 | tf_op jit(solution)/shard_map/all_gather | solution.py:115
  163.2 6.7 %fusion.12 = f32[1,3072,128]{1,2,0:T(8,128)S(1)} fusion(bf16[2048,128]{1,0:T(8,128)(2,1)} %get-tuple-element.9, bf16[1,2048,3072]{2,1,0:T(8,128)(2,1)} %all-gather.3.cloned.1.call-done), kind=kOutput, calls=%fused_computation.10 | convolution fusion | flops 1610612736 | bytes 14680064 | tf_op jit(solution)/shard_map/dot_general | solution.py:17
  169.9 1.6 copy-done.3
  171.5 1.8 fusion.6
  173.3 1.8 fusion.9
  175.1 2.8 pad_maximum_fusion
  177.9 7.0 %copy.29 = f32[3,3072,128]{2,0,1:T(4,128)} copy(f32[3,3072,128]{1,2,0:T(8,128)} %pad_maximum_fusion) | data formatting | bytes 9437184
  184.9 5.6 %copy.34 = f32[384,8,3,128]{3,1,2,0:T(8,128)} copy(f32[384,8,3,128]{3,2,1,0:T(4,128)} %bitcast.68) | data formatting | bytes 9437184
  190.5 20.1 %all_to_all.21 = bf16[16,128,128]{2,1,0:T(8,128)(2,1)S(1)} all-to-all(bf16[16,128,128]{2,1,0:T(8,128)(2,1)S(1)} %bitcast.63), channel_id=1, replica_groups=mesh['dp'=16,'seq'=16] {'seq'}, dimensions={0} | all-to-all | bytes 1048576 | tf_op jit(solution)/shard_map/all_to_all | solution.py:120
  210.6 20.3 %all_to_all.22 = bf16[16,128,128]{2,1,0:T(8,128)(2,1)S(1)} all-to-all(bf16[16,128,128]{2,1,0:T(8,128)(2,1)S(1)} %bitcast.62), channel_id=1, replica_groups=mesh['dp'=16,'seq'=16] {'seq'}, dimensions={0} | all-to-all | bytes 1048576 | tf_op jit(solution)/shard_map/all_to_all | solution.py:120
  230.9 4.6 %all-to-all-start.3 = ((bf16[16,128,128]{2,1,0:T(8,128)(2,1)}), bf16[16,128,128]{2,1,0:T(8,128)(2,1)S(1)}, u32[]{:S(2)}, u32[]{:S(2)}) async-start(bf16[16,128,128]{2,1,0:T(8,128)(2,1)} %bitcast.13), calls=%async_computation.3 | async-start | bytes 1048576 | tf_op jit(solution)/shard_map/all_to_all | solution.py:120
  235.4 0.3 copy.25
  235.8 1.0 reshape.51
  237.1 1.0 reshape.53
  238.2 11.8 %all-to-all-done.3 = bf16[16,128,128]{2,1,0:T(8,128)(2,1)S(1)} async-done(((bf16[16,128,128]{2,1,0:T(8,128)(2,1)}), bf16[16,128,128]{2,1,0:T(8,128)(2,1)S(1)}, u32[]{:S(2)}, u32[]{:S(2)}) %all-to-all-start.3) | async-done | bytes 524320 | tf_op jit(solution)/shard_map/all_to_all | solution.py:120
  250.3 1.0 reshape.55
  251.3 32.9 %reduce-scatter.4.cloned.1.call-done = f32[192,384]{1,0:T(8,128)} async-done(((f32[3072,384]{1,0:T(8,128)}), f32[192,384]{1,0:T(8,128)}) %reduce-scatter.4.cloned.1.call-update) | async-done | bytes 294928
  284.2 1.1 reshape.60
  285.3 0.7 copy.28
  (16 shorter events, 1.3 us)
Async XLA Ops:
  7.2 34.2 %copy-start = (bf16[1,2048,128]{2,1,0:T(8,128)(2,1)S(1)}, bf16[1,2048,128]{2,1,0:T(8,128)(2,1)}, u32[]{:S(2)}) copy-start(bf16[1,2048,128]{2,1,0:T(8,128)(2,1)} %param.7) | copy-start | bytes 1572868
  7.2 34.2 %copy-start.1 = (bf16[1,2048,128]{2,1,0:T(8,128)(2,1)S(1)}, bf16[1,2048,128]{2,1,0:T(8,128)(2,1)}, u32[]{:S(2)}) copy-start(bf16[1,2048,128]{2,1,0:T(8,128)(2,1)} %param.8) | copy-start | bytes 1572868
  7.2 34.2 %copy-start.2 = (bf16[1,2048,128]{2,1,0:T(8,128)(2,1)S(1)}, bf16[1,2048,128]{2,1,0:T(8,128)(2,1)}, u32[]{:S(2)}) copy-start(bf16[1,2048,128]{2,1,0:T(8,128)(2,1)} %param.9) | copy-start | bytes 1572868
  7.2 156.0 %all-gather.3.cloned.1.call-start = ((), (), s32[]{:S(2)}) async-start(), calls=%async_computation.5 | async-start | bytes 13369344 | tf_op jit(solution)/shard_map/all_gather | solution.py:115
  7.9 276.3 %reduce-scatter.4.cloned.1.call-start = ((), (), s32[]{:S(2)}) async-start(), calls=%async_computation.6 | async-start | bytes 5013504
  163.2 8.3 %copy-start.3 = (bf16[1,2048,3072]{2,1,0:T(8,128)(2,1)S(1)}, bf16[1,2048,3072]{2,1,0:T(8,128)(2,1)}, u32[]{:S(2)}) copy-start(bf16[1,2048,3072]{2,1,0:T(8,128)(2,1)} %all-gather.3.cloned.1.call-done) | copy-start | bytes 37748740
  230.9 19.1 %all-to-all-start.3 = ((bf16[16,128,128]{2,1,0:T(8,128)(2,1)}), bf16[16,128,128]{2,1,0:T(8,128)(2,1)S(1)}, u32[]{:S(2)}, u32[]{:S(2)}) async-start(bf16[16,128,128]{2,1,0:T(8,128)(2,1)} %bitcast.13), calls=%async_computation.3 | async-start | bytes 1048576 | tf_op jit(solution)/shard_map/all_to_all | solution.py:120
Sparse Core Ops, SparseCore 0:
  9.8 153.2 all-gather.2
  190.6 93.5 reduce-scatter.3

commit v2 on v1

v2 whole, which is shorter than its diff:
```python
import functools

import jax
import jax.numpy as jnp
from jax import lax
from jax.experimental import pallas as pl
from jax.experimental.pallas import tpu as pltpu
from jax.sharding import PartitionSpec as P

HEAD_DIM = 64
LANES = 128
ROWS = 512
KEYS = 256
OWNERS = 16
RING = 8
ACROSS = 4
HOPS = RING - 1
MESH = pl.DeviceIdType.MESH
f32 = jnp.float32
bf16 = jnp.bfloat16


def dot(a, b, over=((1,), (0,))):
    return lax.dot_general(a, b, (over, ((), ())), preferred_element_type=f32)


def kernel(
    length_ref, payload_ref, factor_ref, q_hbm, k_hbm, v_hbm, inputs_hbm,
    back_q, back_k, back_v, weight_ref,
    q_ref, k_ref, v_ref, u_ref, sent_up, keys, keys_t, scores, weights, grads, key_total, value_total,
    natural, turned, gathered, kept, to_sibling, from_sibling, staged, terms,
    load_sem, up_send, up_recv, swap_send, swap_recv, right_send, right_recv, left_send, left_recv,
    back_send, back_recv, turned_send, turned_recv, sibling_send, sibling_recv, term_send, term_recv,
):
    positions = q_ref.shape[0]
    tokens = payload_ref.shape[0]
    half = gathered.shape[2]
    columns = half // ACROSS
    depth = columns // 2
    backs = (back_q, back_k, back_v)

    clip, me = lax.axis_index("dp"), lax.axis_index("seq")
    y_hi, x, core = clip // (2 * ACROSS), clip // 2 % ACROSS, clip % 2
    y_lo, z = me // RING, me % RING
    partner = {"dp": clip, "seq": (1 - y_lo) * RING + z}
    right = {"dp": clip, "seq": y_lo * RING + (z + 1) % RING}
    left = {"dp": clip, "seq": y_lo * RING + (z + RING - 1) % RING}
    sibling = {"dp": clip + 1 - 2 * core, "seq": me}
    is_self = (y_hi == y_lo) & (y_lo == core)
    quad = me // 4

    def remote(src, dst, send, recv, device):
        return pltpu.make_async_remote_copy(
            src_ref=src, dst_ref=dst, send_sem=send, recv_sem=recv, device_id=device, device_id_type=MESH
        )

    def rows_of(owner):
        return pl.ds(pl.multiple_of(owner * tokens, tokens), tokens)

    def columns_of(owner):
        return pl.ds(pl.multiple_of(owner * LANES, LANES), LANES)

    loads = [
        pltpu.make_async_copy(src, dst, load_sem.at[n])
        for n, (src, dst) in enumerate(((q_hbm, q_ref), (k_hbm, k_ref), (v_hbm, v_ref)))
    ]
    own_columns = pl.ds(pl.multiple_of(y_lo * half, LANES), half)
    other_columns = pl.ds(pl.multiple_of((1 - y_lo) * half, LANES), half)
    loads.append(pltpu.make_async_copy(inputs_hbm.at[:, own_columns], gathered.at[me], load_sem.at[3]))
    for load in loads:
        load.start()

    barrier = pltpu.get_barrier_semaphore()

    def greet(d, _):
        pl.semaphore_signal(barrier, inc=1, device_id={"dp": clip, "seq": (me + d) % OWNERS}, device_id_type=MESH)
        return 0

    lax.fori_loop(1, OWNERS, greet, 0)
    pl.semaphore_signal(barrier, inc=1, device_id=sibling, device_id_type=MESH)

    def greet_source(n, _):
        @pl.when(jnp.logical_not(is_self & (n == y_hi * ACROSS + x)))
        def _():
            source = {"dp": n // ACROSS * (2 * ACROSS) + n % ACROSS * 2 + y_lo, "seq": y_hi * RING + z}
            pl.semaphore_signal(barrier, inc=1, device_id=source, device_id_type=MESH)

        return 0

    lax.fori_loop(0, 2 * ACROSS, greet_source, 0)

    heads = factor_ref.shape[1]
    spread = lax.broadcasted_iota(jnp.int32, (heads, heads * HEAD_DIM), 1) // HEAD_DIM
    spread = (spread == lax.broadcasted_iota(jnp.int32, spread.shape, 0)).astype(f32).astype(bf16)
    token = me * tokens + lax.broadcasted_iota(jnp.int32, (tokens, heads * HEAD_DIM), 0)
    live = jnp.where(token < length_ref[0], 1.0, 0.0)
    sent_up[...] = (payload_ref[...].astype(f32) * dot(factor_ref[...], spread) * live).astype(bf16)

    pl.semaphore_wait(barrier, OWNERS + 2 * ACROSS - jnp.where(is_self, 1, 0))

    def up_copy(peer):
        return remote(
            sent_up.at[:, columns_of(peer)], u_ref.at[rows_of(me), :], up_send.at[peer], up_recv.at[me],
            {"dp": clip, "seq": peer},
        )

    def up_order(n):
        return (quad + 4 - n // 4) % 4 * 4 + (me + n) % 4

    def send_up(n, _):
        up_copy(up_order(n)).start()
        return 0

    own_up = pltpu.make_async_copy(sent_up.at[:, columns_of(me)], u_ref.at[rows_of(me), :], load_sem.at[4])
    own_up.start()
    lax.fori_loop(1, OWNERS, send_up, 0)

    swap = remote(inputs_hbm.at[:, other_columns], gathered.at[me], swap_send, swap_recv, partner)
    swap.start()

    def block_of(kind, place):
        return jnp.where(kind == 0, y_lo, 1 - y_lo) * RING + (place + RING) % RING

    def hop(to, block, k):
        send, recv = (right_send, right_recv) if to is right else (left_send, left_recv)
        return remote(gathered.at[block], gathered.at[block], send.at[k], recv.at[k], to)

    def right_block(k):
        return block_of(k % 2, z - k // 2 - 1)

    def left_block(k):
        return block_of(jnp.where(k == HOPS - 1, 1, k % 2), z + k // 2 + 1)

    def ring_step(k):
        hop(right, right_block(k), k).wait_recv()

        @pl.when(k + 2 < HOPS)
        def _():
            hop(right, right_block(k), k + 2).start()

        hop(left, left_block(k), k).wait_recv()

        @pl.when(k + 2 < HOPS - 1)
        def _():
            hop(left, left_block(k), k + 2).start()

        @pl.when(k == HOPS - 2)
        def _():
            hop(left, left_block(k), HOPS - 1).start()

    loads[3].wait()
    hop(right, me, 0).start()
    hop(left, me, 0).start()

    chunks = [slice(at, at + KEYS) for at in range(0, positions, KEYS)]
    length = length_ref[0]
    position = lax.broadcasted_iota(jnp.int32, (positions, LANES), 0)
    lane = lax.broadcasted_iota(jnp.int32, (positions, LANES), 1)
    keys[:, LANES:] = jnp.where((lane == 0) & (position >= length), -1e30, 0.0).astype(bf16)
    key_total[...] = jnp.zeros_like(key_total)
    value_total[...] = jnp.zeros_like(value_total)
    for load in loads[:3]:
        load.wait()
    keys[:, :LANES] = k_ref[...]
    keys_t[...] = k_ref[...].T
    lane_row = lax.broadcasted_iota(jnp.int32, (ROWS, LANES), 1)
    ones = jnp.where(lane_row == 0, 1.0, 0.0).astype(bf16)
    own_up.wait()
    swap.wait_recv()
    swapped = partner["seq"]
    hop(right, swapped, 1).start()
    hop(left, swapped, 1).start()

    def back_copy(kind, peer):
        return remote(
            natural.at[kind, rows_of(peer), :], backs[kind].at[:, columns_of(me)],
            back_send.at[kind, peer], back_recv.at[kind, me], {"dp": clip, "seq": peer},
        )

    def back_own(kind):
        return pltpu.make_async_copy(
            natural.at[kind, rows_of(me), :], backs[kind].at[:, columns_of(me)], back_send.at[kind, me]
        )


    def turned_quarter(index):
        at = pl.ds(pl.multiple_of(index * ROWS, ROWS), ROWS)
        view = turned.at[y_lo, pl.ds(0, LANES), at]
        return remote(view, view, turned_send.at[index], turned_recv.at[index], partner)

    def turned_rest():
        view = turned.at[y_lo, pl.ds(LANES, 2 * LANES), :]
        return remote(view, view, turned_send.at[4], turned_recv.at[4], partner)

    def block(step, _):
        index = (quad + step) % 4

        def await_up(n, _):
            peer = index * 4 + n

            @pl.when(peer != me)
            def _():
                remote(
                    sent_up.at[:, columns_of(peer)], u_ref.at[rows_of(peer), :], up_send.at[peer], up_recv.at[peer],
                    {"dp": clip, "seq": peer},
                ).wait_recv()

            return 0

        lax.fori_loop(0, 4, await_up, 0)
        start = pl.multiple_of(index * ROWS, ROWS)
        query = q_ref[pl.ds(start, ROWS), :].astype(f32) * HEAD_DIM**-0.5
        upstream = u_ref[pl.ds(start, ROWS), :].astype(f32)
        parts = []
        for head in range(LANES // HEAD_DIM):
            mine = lane_row // HEAD_DIM == head
            q = jnp.where(mine, query, 0.0).astype(bf16)
            u = jnp.where(mine, upstream, 0.0).astype(bf16)
            q_ones = jnp.concatenate([q, ones], axis=1)
            top = jnp.full((8, ROWS), -3e38, f32)
            for chunk in chunks:
                s = dot(keys[chunk, :], q_ones, ((1,), (1,)))
                scores[chunk, :] = s
                top = jnp.maximum(top, jnp.max(s.reshape(KEYS // 8, 8, ROWS), axis=0))
            top = jnp.max(top, axis=0, keepdims=True)
            mass = jnp.zeros((8, ROWS), f32)
            balance = jnp.zeros((8, ROWS), f32)
            for chunk in chunks:
                e = jnp.exp(scores[chunk, :] - top)
                weights[chunk, :] = e
                g = dot(v_ref[chunk, :], u, ((1,), (1,)))
                grads[chunk, :] = g
                mass += jnp.sum(e.reshape(KEYS // 8, 8, ROWS), axis=0)
                balance += jnp.sum((e * g).reshape(KEYS // 8, 8, ROWS), axis=0)
            scale = 1.0 / jnp.sum(mass, axis=0, keepdims=True)
            balance = jnp.sum(balance, axis=0, keepdims=True) * scale
            grad_q = jnp.zeros((HEAD_DIM, ROWS), f32)
            for chunk in chunks:
                p = weights[chunk, :] * scale
                ds = (p * (grads[chunk, :] - balance)).astype(bf16)
                value_total[chunk, :] += dot(p.astype(bf16), u)
                key_total[chunk, :] += dot(ds, q)
                grad_q += dot(keys_t[head * HEAD_DIM : (head + 1) * HEAD_DIM, chunk], ds)
            parts.append(grad_q * HEAD_DIM**-0.5)
        grad_q = jnp.concatenate(parts, axis=0)
        turned[y_lo, 0:LANES, pl.ds(start, ROWS)] = grad_q.astype(bf16)
        natural[0, pl.ds(start, ROWS), :] = grad_q.T.astype(bf16)
        turned_quarter(index).start()

        def send_back(n, _):
            peer = index * 4 + (me + n) % 4

            @pl.when(peer != me)
            def _():
                back_copy(0, peer).start()

            @pl.when(peer == me)
            def _():
                back_own(0).start()

            return 0

        lax.fori_loop(0, 4, send_back, 0)
        ring_step(step)
        return 0

    lax.fori_loop(0, positions // ROWS, block, 0)

    for kind, total in ((1, key_total), (2, value_total)):
        low = total[...].astype(bf16)
        natural[kind] = low
        turned[y_lo, kind * LANES : (kind + 1) * LANES, :] = low.T
    turned_rest().start()
    for k in range(positions // ROWS, HOPS):
        ring_step(jnp.int32(k))

    def send_rest(n, _):
        peer = (me + n) % OWNERS
        back_copy(1, peer).start()
        back_copy(2, peer).start()
        return 0

    back_own(1).start()
    back_own(2).start()
    lax.fori_loop(1, OWNERS, send_rest, 0)

    for index in range(4):
        turned_quarter(index).wait_recv()
    turned_rest().wait_recv()

    def sibling_copy(n):
        return remote(to_sibling.at[n], from_sibling.at[n], sibling_send.at[n], sibling_recv.at[n], sibling)

    def place_of(n):
        return (x + 1 + n) % ACROSS

    def multiply(n, _):
        at = pl.ds(pl.multiple_of(place_of(n) * columns, LANES), columns)
        part = gathered[:, :, at].reshape(positions, columns)
        to_sibling[n] = dot(turned[1 - core], part).astype(bf16)
        sibling_copy(n).start()
        kept[n] = dot(turned[core], part)
        return 0

    lax.fori_loop(0, ACROSS, multiply, 0)

    def term_copy(n, c):
        target = {"dp": y_lo * (2 * ACROSS) + place_of(n) * 2 + c, "seq": core * RING + z}
        slot = y_hi * ACROSS + x
        return remote(
            staged.at[n, pl.ds(c * depth, depth), :], terms.at[slot], term_send.at[n, c], term_recv.at[slot], target
        )

    def term_own(c):
        return pltpu.make_async_copy(
            staged.at[ACROSS - 1, pl.ds(c * depth, depth), :], terms.at[y_hi * ACROSS + x], term_recv.at[y_hi * ACROSS + x]
        )

    def reduce(n, _):
        sibling_copy(n).wait_recv()
        staged[n] = (kept[n] + from_sibling[n].astype(f32)).T.astype(bf16)
        for c in range(2):
            own = is_self & (n == ACROSS - 1) & (core == c)

            @pl.when(jnp.logical_not(own))
            def _():
                term_copy(n, c).start()

            @pl.when(own)
            def _():
                term_own(c).start()

        return 0

    lax.fori_loop(0, ACROSS, reduce, 0)

    def await_term(n, _):
        pltpu.make_async_copy(terms.at[n], terms.at[n], term_recv.at[n]).wait()
        return 0

    lax.fori_loop(0, 2 * ACROSS, await_term, 0)
    total = terms[0].astype(f32)
    for n in range(1, 2 * ACROSS):
        total += terms[n].astype(f32)
    for kind in range(3):
        weight_ref[kind] = total[:, kind * LANES : (kind + 1) * LANES]

    def await_back(peer, _):
        @pl.when(peer != me)
        def _():
            for kind in range(3):
                remote(
                    natural.at[kind, rows_of(peer), :], backs[kind].at[:, columns_of(peer)],
                    back_send.at[kind, peer], back_recv.at[kind, peer], {"dp": clip, "seq": peer},
                ).wait()
            up_copy(peer).wait_send()

        return 0

    lax.fori_loop(0, OWNERS, await_back, 0)
    for kind in range(3):
        back_own(kind).wait()
    swap.wait_send()
    for k in range(HOPS):
        hop(right, me, k).wait_send()
        hop(left, me, k).wait_send()
    for index in range(4):
        turned_quarter(index).wait_send()
    turned_rest().wait_send()

    def await_sent(n, _):
        sibling_copy(n).wait_send()
        for c in range(2):
            @pl.when(jnp.logical_not(is_self & (n == ACROSS - 1) & (core == c)))
            def _():
                term_copy(n, c).wait_send()

        return 0

    lax.fori_loop(0, ACROSS, await_sent, 0)


def shards(queries, key_states, value_states, grad_payload, grad_scale, inputs, lengths):
    _, positions, width = queries.shape
    _, rows, features = grad_payload.shape
    model = inputs.shape[2]
    half = model // 2
    columns = half // ACROSS
    dma, vmem = pltpu.SemaphoreType.DMA, pltpu.VMEM
    whole = pl.BlockSpec(memory_space=pltpu.VMEM)
    anywhere = pl.BlockSpec(memory_space=pl.ANY)
    *back, weight_grad = pl.pallas_call(
        kernel,
        out_shape=[jax.ShapeDtypeStruct((rows, features), bf16)] * 3
        + [jax.ShapeDtypeStruct((3, columns // 2, width), f32)],
        in_specs=[pl.BlockSpec(memory_space=pltpu.SMEM), whole, whole] + [anywhere] * 4,
        out_specs=[anywhere] * 3 + [whole],
        scratch_shapes=[vmem((positions, width), bf16)] * 4
        + [
            vmem((rows, features), bf16),
            vmem((positions, 2 * width), bf16),
            vmem((width, positions), bf16),
            vmem((positions, ROWS), f32),
            vmem((positions, ROWS), f32),
            vmem((positions, ROWS), f32),
            vmem((positions, width), f32),
            vmem((positions, width), f32),
            vmem((3, positions, width), bf16),
            vmem((2, 3 * width, positions), bf16),
            vmem((OWNERS, rows, half), bf16),
            vmem((ACROSS, 3 * width, columns), f32),
            vmem((ACROSS, 3 * width, columns), bf16),
            vmem((ACROSS, 3 * width, columns), bf16),
            vmem((ACROSS, columns, 3 * width), bf16),
            vmem((2 * ACROSS, columns // 2, 3 * width), bf16),
            dma((5,)),
            dma((OWNERS,)),
            dma((OWNERS,)),
            dma,
            dma,
            dma((HOPS,)),
            dma((HOPS,)),
            dma((HOPS,)),
            dma((HOPS,)),
            dma((3, OWNERS)),
            dma((3, OWNERS)),
            dma((5,)),
            dma((5,)),
            dma((ACROSS,)),
            dma((ACROSS,)),
            dma((ACROSS, 2)),
            dma((2 * ACROSS,)),
        ],
        compiler_params=pltpu.CompilerParams(
            collective_id=0, has_side_effects=True, vmem_limit_bytes=56 * 2**20
        ),
        name="attention_and_weights",
    )(lengths, grad_payload[0], grad_scale[0], queries[0], key_states[0], value_states[0], inputs[0])
    return (*[grad[None] for grad in back], weight_grad)


def solution(mesh):
    return jax.shard_map(
        shards,
        mesh=mesh,
        in_specs=(
            P("dp", None, "seq"),
            P("dp", None, "seq"),
            P("dp", None, "seq"),
            P("dp", "seq", None),
            P("dp", "seq", None),
            P("dp", "seq", None),
            P("dp"),
        ),
        out_specs=(
            P("dp", "seq", None),
            P("dp", "seq", None),
            P("dp", "seq", None),
            P(None, "dp", "seq"),
        ),
        check_vma=False,
    )
```

time: 293 us -> 138 us (0.47)
  the two profiles are of different devices: /device:TPU:2 before, /device:TPU:249 now
where the time goes in v2:
time: 138 us
  Pallas kernels  131 us (95%)
  local copies, waits for them, and re-layouts  5.76 us (4%)
    pallas_call x1, Pallas kernels, shards(): pl.pallas_call(kernel, out_shape=[jax.ShapeDtypeStruct((rows, features),...  131 us
    unnamed x13, local copies, waits for them, and re-layouts  5.76 us

profile of v2, /device:TPU:249, one launch (start us, length us, event | category | flops | bytes accessed | tf_op | source)
XLA Modules:
  0.0 137.8 jit_solution(8886060441619202137)
XLA Ops:
  0.6 0.0 copy-start.3
  1.3 0.0 copy-done.3
  1.3 0.7 copy.11
  2.1 130.7 %attention_and_weights.1 = (bf16[128,2048]{1,0:T(8,128)(2,1)}, bf16[128,2048]{1,0:T(8,128)(2,1)}, bf16[128,2048]{1,0:T(8,128)(2,1)}, f32[3,192,128]{2,1,0:T(8,128)}) custom-call(s32[1]{0:T(128)S(6)} %copy.16.length_ref, bf16[128,2048]{1,0:T(8,128)(2,1)} %bitcast.10, bf16[128,32]{1,0:T(8,128)(2,1)} %bitcast.17, bf16[2048,128]{1,0:T(8,128)(2,1)} %bitcast.11, ...), custom_call_target="tpu_custom_call" | custom-call | tf_op jit(solution)/shard_map/attention_and_weights/pallas_call | solution.py:392
  132.8 0.0 copy-start.1
  132.8 1.9 %copy.17 = bf16[1,128,2048]{2,1,0:T(8,128)(2,1)} copy(bf16[1,128,2048]{2,1,0:T(8,128)(2,1)} %bitcast.16) | data formatting | bytes 1048576
  134.7 0.0 copy-done.1
  134.7 0.0 copy-start
  134.7 0.8 copy.18
  135.5 0.4 copy-done
  136.0 0.0 copy-start.2
  136.0 0.8 copy.19
  136.8 0.3 copy-done.2
  137.1 0.7 copy.20
Async XLA Ops:
  0.6 0.7 copy-start.3
  132.8 2.0 %copy-start.1 = (bf16[128,2048]{1,0:T(8,128)(2,1)S(1)}, bf16[128,2048]{1,0:T(8,128)(2,1)}, u32[]{:S(2)}) copy-start(bf16[128,2048]{1,0:T(8,128)(2,1)} %get-tuple-element.9) | copy-start | bytes 1572868
  134.7 1.2 copy-start
  136.0 1.1 copy-start.2

commit v3 on v2

v3 whole, which is shorter than its diff:
```python
import functools

import jax
import jax.numpy as jnp
from jax import lax
from jax.experimental import pallas as pl
from jax.experimental.pallas import tpu as pltpu
from jax.sharding import PartitionSpec as P

HEAD_DIM = 64
LANES = 128
ROWS = 512
KEYS = 256
OWNERS = 16
RING = 8
ACROSS = 4
HOPS = RING - 1
MESH = pl.DeviceIdType.MESH
f32 = jnp.float32
bf16 = jnp.bfloat16


def dot(a, b, over=((1,), (0,))):
    return lax.dot_general(a, b, (over, ((), ())), preferred_element_type=f32)


def kernel(
    length_ref, payload_ref, factor_ref, q_hbm, k_hbm, v_hbm, inputs_hbm,
    back_q, back_k, back_v, weight_ref,
    q_ref, k_ref, v_ref, u_ref, sent_up, keys, keys_t, scores, weights, grads, key_total, value_total,
    natural, turned, gathered, weight_total, to_sibling, from_sibling, staged, from_x, leaving, terms,
    load_sem, up_send, up_recv, swap_send, swap_recv, right_send, right_recv, left_send, left_recv,
    back_send, back_recv, turned_send, turned_recv, sibling_send, sibling_recv, sum_send, sum_recv, term_send, term_recv,
):
    positions = q_ref.shape[0]
    tokens = payload_ref.shape[0]
    half = gathered.shape[2]
    columns = half // ACROSS
    depth = columns // 2
    backs = (back_q, back_k, back_v)

    clip, me = lax.axis_index("dp"), lax.axis_index("seq")
    y_hi, x, core = clip // (2 * ACROSS), clip // 2 % ACROSS, clip % 2
    y_lo, z = me // RING, me % RING
    partner = {"dp": clip, "seq": (1 - y_lo) * RING + z}
    right = {"dp": clip, "seq": y_lo * RING + (z + 1) % RING}
    left = {"dp": clip, "seq": y_lo * RING + (z + RING - 1) % RING}
    sibling = {"dp": clip + 1 - 2 * core, "seq": me}

    def along_x(by):
        return {"dp": clip + 2 * ((x + ACROSS + by) % ACROSS - x), "seq": me}

    is_self = (y_hi == y_lo) & (y_lo == core)
    quad = me // 4

    def remote(src, dst, send, recv, device):
        return pltpu.make_async_remote_copy(
            src_ref=src, dst_ref=dst, send_sem=send, recv_sem=recv, device_id=device, device_id_type=MESH
        )

    def rows_of(owner):
        return pl.ds(pl.multiple_of(owner * tokens, tokens), tokens)

    def columns_of(owner):
        return pl.ds(pl.multiple_of(owner * LANES, LANES), LANES)

    loads = [
        pltpu.make_async_copy(src, dst, load_sem.at[n])
        for n, (src, dst) in enumerate(((q_hbm, q_ref), (k_hbm, k_ref), (v_hbm, v_ref)))
    ]
    own_columns = pl.ds(pl.multiple_of(y_lo * half, LANES), half)
    other_columns = pl.ds(pl.multiple_of((1 - y_lo) * half, LANES), half)
    loads.append(pltpu.make_async_copy(inputs_hbm.at[:, own_columns], gathered.at[me], load_sem.at[3]))
    for load in loads:
        load.start()

    barrier = pltpu.get_barrier_semaphore()

    def greet(d, _):
        pl.semaphore_signal(barrier, inc=1, device_id={"dp": clip, "seq": (me + d) % OWNERS}, device_id_type=MESH)
        return 0

    lax.fori_loop(1, OWNERS, greet, 0)
    pl.semaphore_signal(barrier, inc=1, device_id=sibling, device_id_type=MESH)

    for n in range(ACROSS - 1):
        pl.semaphore_signal(barrier, inc=1, device_id=along_x(-1 - n), device_id_type=MESH)
    for n in range(2):
        @pl.when(jnp.logical_not(is_self & (n == y_hi)))
        def _(n=n):
            source = {"dp": n * (2 * ACROSS) + x * 2 + y_lo, "seq": y_hi * RING + z}
            pl.semaphore_signal(barrier, inc=1, device_id=source, device_id_type=MESH)

    pl.semaphore_wait(barrier, OWNERS + ACROSS + 1 - jnp.where(is_self, 1, 0))

    swap = remote(inputs_hbm.at[:, other_columns], gathered.at[me], swap_send, swap_recv, partner)
    swap.start()

    def block_of(kind, place):
        return jnp.where(kind == 0, y_lo, 1 - y_lo) * RING + (place + RING) % RING

    def hop(to, block, k, src=None):
        send, recv = (right_send, right_recv) if to is right else (left_send, left_recv)
        return remote(gathered.at[block] if src is None else src, gathered.at[block], send.at[k], recv.at[k], to)

    def right_block(k):
        return block_of(k % 2, z - k // 2 - 1)

    def left_block(k):
        return block_of(jnp.where(k == HOPS - 1, 1, k % 2), z + k // 2 + 1)

    def ring_step(k):
        hop(right, right_block(k), k).wait_recv()

        @pl.when(k + 2 < HOPS)
        def _():
            hop(right, right_block(k), k + 2).start()

        hop(left, left_block(k), k).wait_recv()

        @pl.when(k + 2 < HOPS - 1)
        def _():
            hop(left, left_block(k), k + 2).start()

        @pl.when(k == HOPS - 2)
        def _():
            hop(left, left_block(k), HOPS - 1).start()

    own_input = inputs_hbm.at[:, own_columns]
    hop(right, me, 0, own_input).start()
    hop(left, me, 0, own_input).start()

    heads = factor_ref.shape[0]
    spread = lax.broadcasted_iota(jnp.int32, (heads, heads * HEAD_DIM), 1) // HEAD_DIM
    spread = (spread == lax.broadcasted_iota(jnp.int32, spread.shape, 0)).astype(f32).astype(bf16)
    token = me * tokens + lax.broadcasted_iota(jnp.int32, (tokens, heads * HEAD_DIM), 0)
    live = jnp.where(token < length_ref[0], 1.0, 0.0)
    sent_up[...] = (payload_ref[...].astype(f32) * dot(factor_ref[...], spread, ((0,), (0,))) * live).astype(bf16)

    def up_copy(peer):
        return remote(
            sent_up.at[:, columns_of(peer)], u_ref.at[rows_of(me), :], up_send.at[peer], up_recv.at[me],
            {"dp": clip, "seq": peer},
        )

    def up_order(n):
        return (quad + 4 - n // 4) % 4 * 4 + (me + n) % 4

    def send_up(n, _):
        up_copy(up_order(n)).start()
        return 0

    own_up = pltpu.make_async_copy(sent_up.at[:, columns_of(me)], u_ref.at[rows_of(me), :], load_sem.at[4])
    own_up.start()
    lax.fori_loop(1, OWNERS, send_up, 0)

    chunks = [slice(at, at + KEYS) for at in range(0, positions, KEYS)]
    length = length_ref[0]
    position = lax.broadcasted_iota(jnp.int32, (positions, LANES), 0)
    lane = lax.broadcasted_iota(jnp.int32, (positions, LANES), 1)
    keys[:, LANES:] = jnp.where((lane == 0) & (position >= length), -1e30, 0.0).astype(bf16)
    key_total[...] = jnp.zeros_like(key_total)
    value_total[...] = jnp.zeros_like(value_total)
    for load in loads:
        load.wait()
    keys[:, :LANES] = k_ref[...]
    keys_t[...] = k_ref[...].T
    lane_row = lax.broadcasted_iota(jnp.int32, (ROWS, LANES), 1)
    ones = jnp.where(lane_row == 0, 1.0, 0.0).astype(bf16)
    own_up.wait()
    swap.wait_recv()
    swapped = partner["seq"]
    hop(right, swapped, 1).start()
    hop(left, swapped, 1).start()

    def back_copy(kind, peer):
        return remote(
            natural.at[kind, rows_of(peer), :], backs[kind].at[:, columns_of(me)],
            back_send.at[kind, peer], back_recv.at[kind, me], {"dp": clip, "seq": peer},
        )

    def back_own(kind):
        return pltpu.make_async_copy(
            natural.at[kind, rows_of(me), :], backs[kind].at[:, columns_of(me)], back_send.at[kind, me]
        )


    def turned_copy(kind, head):
        view = turned.at[y_lo, pl.ds(kind * LANES + head * HEAD_DIM, HEAD_DIM), :]
        return remote(view, view, turned_send.at[kind, head], turned_recv.at[kind, head], partner)

    def block(unit, _):
        head, step = unit // 4, unit % 4
        index = (quad + step) % 4

        def await_up(n, _):
            peer = index * 4 + n

            @pl.when(peer != me)
            def _():
                remote(
                    sent_up.at[:, columns_of(peer)], u_ref.at[rows_of(peer), :], up_send.at[peer], up_recv.at[peer],
                    {"dp": clip, "seq": peer},
                ).wait_recv()

            return 0

        @pl.when(head == 0)
        def _():
            lax.fori_loop(0, 4, await_up, 0)

        start = pl.multiple_of(index * ROWS, ROWS)
        mine = lane_row // HEAD_DIM == head
        q = jnp.where(mine, q_ref[pl.ds(start, ROWS), :].astype(f32) * HEAD_DIM**-0.5, 0.0).astype(bf16)
        u = jnp.where(mine, u_ref[pl.ds(start, ROWS), :].astype(f32), 0.0).astype(bf16)
        q_ones = jnp.concatenate([q, ones], axis=1)
        top = jnp.full((8, ROWS), -3e38, f32)
        for chunk in chunks:
            s = dot(keys[chunk, :], q_ones, ((1,), (1,)))
            scores[chunk, :] = s
            top = jnp.maximum(top, jnp.max(s.reshape(KEYS // 8, 8, ROWS), axis=0))
        top = jnp.max(top, axis=0, keepdims=True)
        mass = jnp.zeros((8, ROWS), f32)
        balance = jnp.zeros((8, ROWS), f32)
        for chunk in chunks:
            e = jnp.exp(scores[chunk, :] - top)
            weights[chunk, :] = e
            g = dot(v_ref[chunk, :], u, ((1,), (1,)))
            grads[chunk, :] = g
            mass += jnp.sum(e.reshape(KEYS // 8, 8, ROWS), axis=0)
            balance += jnp.sum((e * g).reshape(KEYS // 8, 8, ROWS), axis=0)
        scale = 1.0 / jnp.sum(mass, axis=0, keepdims=True)
        balance = jnp.sum(balance, axis=0, keepdims=True) * scale
        grad_q = jnp.zeros((HEAD_DIM, ROWS), f32)
        head_rows = pl.ds(pl.multiple_of(head * HEAD_DIM, HEAD_DIM), HEAD_DIM)
        for chunk in chunks:
            p = weights[chunk, :] * scale
            ds = (p * (grads[chunk, :] - balance)).astype(bf16)
            value_total[chunk, :] += dot(p.astype(bf16), u)
            key_total[chunk, :] += dot(ds, q)
            grad_q += dot(keys_t[head_rows, chunk], ds)
        turned[y_lo, head_rows, pl.ds(start, ROWS)] = (grad_q * HEAD_DIM**-0.5).astype(bf16)

        @pl.when((unit >= 3) & (unit % 2 == 1))
        def _():
            ring_step((unit - 3) // 2)

        @pl.when(step == 3)
        def _():
            turned_copy(0, head).start()
            for kind, total in ((1, key_total), (2, value_total)):
                flat = total[...].astype(bf16).T
                turned[y_lo, pl.ds(pl.multiple_of(kind * LANES + head * HEAD_DIM, HEAD_DIM), HEAD_DIM), :] = jnp.where(
                    head == 0, flat[:HEAD_DIM].astype(f32), flat[HEAD_DIM:].astype(f32)
                ).astype(bf16)
                turned_copy(kind, head).start()

        return 0

    units = positions // ROWS * (LANES // HEAD_DIM)
    lax.fori_loop(0, units, block, 0)

    natural[1] = key_total[...].astype(bf16)
    natural[2] = value_total[...].astype(bf16)
    natural[0] = turned[y_lo, 0:LANES, :].T

    def send_back(kind):
        def send(n, _):
            back_copy(kind, (me + n) % OWNERS).start()
            return 0

        back_own(kind).start()
        lax.fori_loop(1, OWNERS, send, 0)

    def places(sides):
        return [(z + RING + side) % RING for side in sides]

    def product(side, zs, at):
        own = [y * RING + place for place in zs for y in range(2)]
        left_part = jnp.concatenate([turned[side, :, rows_of(block)] for block in own], axis=1)
        return dot(left_part, jnp.concatenate([gathered[block, :, at] for block in own], axis=0))

    def add(side, zs):
        for at in range(0, half, columns):
            weight_total[side, :, at : at + columns] += product(side, zs, slice(at, at + columns))

    def add_pair(side):
        def body(d, _):
            add(side, places((-d, d)))
            return 0

        return body

    def sibling_copy(n):
        return remote(to_sibling.at[n], from_sibling.at[n], sibling_send.at[n], sibling_recv.at[n], sibling)

    def finished(side, n):
        at = pl.ds(pl.multiple_of((x + 1 + n) % ACROSS * columns, LANES), columns)
        return weight_total[side, :, at] + product(side, places((RING // 2,)), at)

    weight_total[...] = jnp.zeros_like(weight_total)
    ring_step(jnp.int32(HOPS - 4))
    add(y_lo, places((0,)))
    lax.fori_loop(1, 3, add_pair(y_lo), 0)
    ring_step(jnp.int32(HOPS - 3))
    ring_step(jnp.int32(HOPS - 2))
    send_back(0)
    add_pair(y_lo)(3, 0)
    for kind in range(3):
        for head in range(2):
            turned_copy(kind, head).wait_recv()
    add(1 - y_lo, places((0,)))
    lax.fori_loop(1, 4, add_pair(1 - y_lo), 0)
    ring_step(jnp.int32(HOPS - 1))

    def give(n, _):
        to_sibling[n] = finished(1 - core, n).astype(bf16)
        sibling_copy(n).start()
        return 0

    lax.fori_loop(0, ACROSS, give, 0)

    def sum_copy(n):
        return remote(staged.at[n], from_x.at[n], sum_send.at[n], sum_recv.at[n], along_x(1 + n))

    def reduce(n, _):
        part = finished(core, n)
        sibling_copy(n).wait_recv()
        staged[n] = (part + from_sibling[n].astype(f32)).astype(bf16)
        sum_copy(n).start()
        return 0

    last = ACROSS - 1
    lax.fori_loop(0, last, reduce, 0)
    send_back(1)
    send_back(2)
    total = finished(core, last)
    sibling_copy(last).wait_recv()
    total += from_sibling[last].astype(f32)
    for n in range(last):
        sum_copy(n).wait_recv()
        total += from_x[n].astype(f32)
    leaving[...] = total.T.astype(bf16)

    def term_copy(c):
        target = {"dp": y_lo * (2 * ACROSS) + x * 2 + c, "seq": core * RING + z}
        return remote(leaving.at[pl.ds(c * depth, depth), :], terms.at[y_hi], term_send.at[c], term_recv.at[y_hi], target)

    def term_own(c):
        return pltpu.make_async_copy(leaving.at[pl.ds(c * depth, depth), :], terms.at[y_hi], term_recv.at[y_hi])

    for c in range(2):
        @pl.when(jnp.logical_not(is_self & (core == c)))
        def _(c=c):
            term_copy(c).start()

        @pl.when(is_self & (core == c))
        def _(c=c):
            term_own(c).start()

    for n in range(2):
        pltpu.make_async_copy(terms.at[n], terms.at[n], term_recv.at[n]).wait()
    total = terms[0].astype(f32) + terms[1].astype(f32)
    for kind in range(3):
        weight_ref[kind] = total[:, kind * LANES : (kind + 1) * LANES]

    def await_back(peer, _):
        @pl.when(peer != me)
        def _():
            for kind in range(3):
                remote(
                    natural.at[kind, rows_of(peer), :], backs[kind].at[:, columns_of(peer)],
                    back_send.at[kind, peer], back_recv.at[kind, peer], {"dp": clip, "seq": peer},
                ).wait()
            up_copy(peer).wait_send()

        return 0

    lax.fori_loop(0, OWNERS, await_back, 0)
    for kind in range(3):
        back_own(kind).wait()
    swap.wait_send()
    for k in range(HOPS):
        hop(right, me, k).wait_send()
        hop(left, me, k).wait_send()
    for kind in range(3):
        for head in range(2):
            turned_copy(kind, head).wait_send()

    for n in range(ACROSS):
        sibling_copy(n).wait_send()
    for n in range(last):
        sum_copy(n).wait_send()
    for c in range(2):
        @pl.when(jnp.logical_not(is_self & (core == c)))
        def _(c=c):
            term_copy(c).wait_send()


def copy_out(*refs):
    count = len(refs) // 2
    copies = [
        pltpu.make_async_copy(src, dst, refs[-1].at[n])
        for n, (src, dst) in enumerate(zip(refs[:count], refs[count:-1]))
    ]
    for copy in copies:
        copy.start()
    for copy in copies:
        copy.wait()


def shards(queries, key_states, value_states, grad_payload, grad_scale, inputs, lengths):
    _, positions, width = queries.shape
    _, rows, features = grad_payload.shape
    model = inputs.shape[2]
    half = model // 2
    columns = half // ACROSS
    dma, vmem = pltpu.SemaphoreType.DMA, pltpu.VMEM
    whole = pl.BlockSpec(memory_space=pltpu.VMEM)
    anywhere = pl.BlockSpec(memory_space=pl.ANY)
    results = pl.pallas_call(
        kernel,
        out_shape=[jax.ShapeDtypeStruct((rows, features), bf16)] * 3
        + [jax.ShapeDtypeStruct((3, columns // 2, width), f32)],
        in_specs=[pl.BlockSpec(memory_space=pltpu.SMEM), whole, whole] + [anywhere] * 4,
        out_specs=[anywhere] * 3 + [whole],
        scratch_shapes=[vmem((positions, width), bf16)] * 4
        + [
            vmem((rows, features), bf16),
            vmem((positions, 2 * width), bf16),
            vmem((width, positions), bf16),
            vmem((positions, ROWS), f32),
            vmem((positions, ROWS), f32),
            vmem((positions, ROWS), f32),
            vmem((positions, width), f32),
            vmem((positions, width), f32),
            vmem((3, positions, width), bf16),
            vmem((2, 3 * width, positions), bf16),
            vmem((OWNERS, rows, half), bf16),
            vmem((2, 3 * width, half), f32),
            vmem((ACROSS, 3 * width, columns), bf16),
            vmem((ACROSS, 3 * width, columns), bf16),
            vmem((ACROSS - 1, 3 * width, columns), bf16),
            vmem((ACROSS - 1, 3 * width, columns), bf16),
            vmem((columns, 3 * width), bf16),
            vmem((2, columns // 2, 3 * width), bf16),
            dma((5,)),
            dma((OWNERS,)),
            dma((OWNERS,)),
            dma,
            dma,
            dma((HOPS,)),
            dma((HOPS,)),
            dma((HOPS,)),
            dma((HOPS,)),
            dma((3, OWNERS)),
            dma((3, OWNERS)),
            dma((3, 2)),
            dma((3, 2)),
            dma((ACROSS,)),
            dma((ACROSS,)),
            dma((ACROSS - 1,)),
            dma((ACROSS - 1,)),
            dma((2,)),
            dma((2,)),
        ],
        compiler_params=pltpu.CompilerParams(
            collective_id=0, has_side_effects=True, vmem_limit_bytes=56 * 2**20
        ),
        name="attention_and_weights",
    )(lengths, grad_payload[0], grad_scale[0].T, queries[0], key_states[0], value_states[0], inputs[0])
    *back, weight_grad = pl.pallas_call(
        copy_out,
        out_shape=[jax.ShapeDtypeStruct(r.shape, r.dtype) for r in results],
        in_specs=[whole] * 4,
        out_specs=[anywhere] * 4,
        scratch_shapes=[dma((4,))],
        name="results",
    )(*results)
    return (*[grad[None] for grad in back], weight_grad)


def solution(mesh):
    return jax.shard_map(
        shards,
        mesh=mesh,
        in_specs=(
            P("dp", None, "seq"),
            P("dp", None, "seq"),
            P("dp", None, "seq"),
            P("dp", "seq", None),
            P("dp", "seq", None),
            P("dp", "seq", None),
            P("dp"),
        ),
        out_specs=(
            P("dp", "seq", None),
            P("dp", "seq", None),
            P("dp", "seq", None),
            P(None, "dp", "seq"),
        ),
        check_vma=False,
    )
```

time: 138 us -> 125 us (0.906)
  the two profiles are of different devices: /device:TPU:249 before, /device:TPU:2 now
where the time goes in v3:
time: 125 us; the launch traced here: 124 us
  Pallas kernels  122 us (98%)
  between operations  1.29 us (1%)
    pallas_call x1, Pallas kernels, shards(): pl.pallas_call(kernel, out_shape=[jax.ShapeDtypeStruct((rows, features),...  120 us
    pallas_call x1, Pallas kernels, shards(): pl.pallas_call(copy_out, out_shape=[jax.ShapeDtypeStruct(r.shape, r.dtype...  2.7 us

profile of v3, /device:TPU:2, one launch (start us, length us, event | category | flops | bytes accessed | tf_op | source)
XLA Modules:
  0.0 123.6 jit_solution(5712290009625383862)
XLA Ops:
  1.3 119.6 %attention_and_weights.1 = (bf16[128,2048]{1,0:T(8,128)(2,1)}, bf16[128,2048]{1,0:T(8,128)(2,1)}, bf16[128,2048]{1,0:T(8,128)(2,1)}, f32[3,192,128]{2,1,0:T(8,128)}) custom-call(s32[1]{0:T(128)S(6)} %copy.11.length_ref, bf16[128,2048]{1,0:T(8,128)(2,1)} %bitcast.12, bf16[32,128]{1,0:T(8,128)(2,1)} %bitcast.16, bf16[2048,128]{1,0:T(8,128)(2,1)} %bitcast.13, ...), custom_call_target="tpu_custom_call" | custom-call | tf_op jit(solution)/shard_map/attention_and_weights/pallas_call | solution.py:421
  120.9 2.7 %results.1 = (bf16[128,2048]{1,0:T(8,128)(2,1)}, bf16[128,2048]{1,0:T(8,128)(2,1)}, bf16[128,2048]{1,0:T(8,128)(2,1)}, f32[3,192,128]{2,1,0:T(8,128)}) custom-call(bf16[128,2048]{1,0:T(8,128)(2,1)} %get-tuple-element.12.refs_0_, bf16[128,2048]{1,0:T(8,128)(2,1)} %get-tuple-element.13.refs_1_, bf16[128,2048]{1,0:T(8,128)(2,1)} %get-tuple-element.14.refs_2_, ...), custom_call_target="tpu_custom_call" | custom-call | tf_op jit(solution)/shard_map/results/pallas_call | solution.py:472

commit v4 on v3

--- a/solution.py
+++ b/solution.py
@@ -28,9 +28,9 @@
     length_ref, payload_ref, factor_ref, q_hbm, k_hbm, v_hbm, inputs_hbm,
     back_q, back_k, back_v, weight_ref,
     q_ref, k_ref, v_ref, u_ref, sent_up, keys, keys_t, scores, weights, grads, key_total, value_total,
-    natural, turned, gathered, weight_total, to_sibling, from_sibling, staged, from_x, leaving, terms,
+    natural, turned, gathered, weight_total, to_sibling, from_sibling, staged, from_x, own_total, leaving, terms,
     load_sem, up_send, up_recv, swap_send, swap_recv, right_send, right_recv, left_send, left_recv,
-    back_send, back_recv, turned_send, turned_recv, sibling_send, sibling_recv, sum_send, sum_recv, term_send, term_recv,
+    back_send, back_recv, turned_send, turned_recv, block_send, block_recv, sibling_send, sibling_recv, sum_send, sum_recv, term_send, term_recv,
 ):
     positions = q_ref.shape[0]
     tokens = payload_ref.shape[0]
@@ -184,6 +184,11 @@
             natural.at[kind, rows_of(me), :], backs[kind].at[:, columns_of(me)], back_send.at[kind, me]
         )
 
+
+    def turned_block(head, index):
+        rows = pl.ds(pl.multiple_of(head * HEAD_DIM, HEAD_DIM), HEAD_DIM)
+        view = turned.at[y_lo, rows, pl.ds(pl.multiple_of(index * ROWS, ROWS), ROWS)]
+        return remote(view, view, block_send.at[head, index], block_recv.at[head, index], partner)
 
     def turned_copy(kind, head):
         view = turned.at[y_lo, pl.ds(kind * LANES + head * HEAD_DIM, HEAD_DIM), :]
@@ -240,14 +245,14 @@
             key_total[chunk, :] += dot(ds, q)
             grad_q += dot(keys_t[head_rows, chunk], ds)
         turned[y_lo, head_rows, pl.ds(start, ROWS)] = (grad_q * HEAD_DIM**-0.5).astype(bf16)
-
-        @pl.when((unit >= 3) & (unit % 2 == 1))
-        def _():
-            ring_step((unit - 3) // 2)
+        turned_block(head, index).start()
+
+        @pl.when((unit >= 2) & (unit % 2 == 0))
+        def _():
+            ring_step((unit - 2) // 2)
 
         @pl.when(step == 3)
         def _():
-            turned_copy(0, head).start()
             for kind, total in ((1, key_total), (2, value_total)):
                 flat = total[...].astype(bf16).T
                 turned[y_lo, pl.ds(pl.multiple_of(kind * LANES + head * HEAD_DIM, HEAD_DIM), HEAD_DIM), :] = jnp.where(
@@ -259,6 +264,7 @@
 
     units = positions // ROWS * (LANES // HEAD_DIM)
     lax.fori_loop(0, units, block, 0)
+    ring_step(jnp.int32(HOPS - 4))
 
     natural[1] = key_total[...].astype(bf16)
     natural[2] = value_total[...].astype(bf16)
@@ -299,15 +305,16 @@
         return weight_total[side, :, at] + product(side, places((RING // 2,)), at)
 
     weight_total[...] = jnp.zeros_like(weight_total)
-    ring_step(jnp.int32(HOPS - 4))
     add(y_lo, places((0,)))
     lax.fori_loop(1, 3, add_pair(y_lo), 0)
     ring_step(jnp.int32(HOPS - 3))
     ring_step(jnp.int32(HOPS - 2))
     send_back(0)
     add_pair(y_lo)(3, 0)
-    for kind in range(3):
-        for head in range(2):
+    for head in range(2):
+        for index in range(4):
+            turned_block(head, index).wait_recv()
+        for kind in range(1, 3):
             turned_copy(kind, head).wait_recv()
     add(1 - y_lo, places((0,)))
     lax.fori_loop(1, 4, add_pair(1 - y_lo), 0)
@@ -320,49 +327,61 @@
 
     lax.fori_loop(0, ACROSS, give, 0)
 
-    def sum_copy(n):
-        return remote(staged.at[n], from_x.at[n], sum_send.at[n], sum_recv.at[n], along_x(1 + n))
+    def sum_copy(kind, n):
+        rows = pl.ds(kind * LANES, LANES)
+        return remote(
+            staged.at[n, rows, :], from_x.at[n, rows, :], sum_send.at[kind, n], sum_recv.at[kind, n], along_x(1 + n)
+        )
 
     def reduce(n, _):
         part = finished(core, n)
         sibling_copy(n).wait_recv()
         staged[n] = (part + from_sibling[n].astype(f32)).astype(bf16)
-        sum_copy(n).start()
         return 0
 
     last = ACROSS - 1
     lax.fori_loop(0, last, reduce, 0)
+    for kind in range(3):
+        for n in range(last):
+            sum_copy(kind, n).start()
     send_back(1)
     send_back(2)
     total = finished(core, last)
     sibling_copy(last).wait_recv()
-    total += from_sibling[last].astype(f32)
-    for n in range(last):
-        sum_copy(n).wait_recv()
-        total += from_x[n].astype(f32)
-    leaving[...] = total.T.astype(bf16)
-
-    def term_copy(c):
+    own_total[...] = total + from_sibling[last].astype(f32)
+
+    def term_copy(kind, c):
         target = {"dp": y_lo * (2 * ACROSS) + x * 2 + c, "seq": core * RING + z}
-        return remote(leaving.at[pl.ds(c * depth, depth), :], terms.at[y_hi], term_send.at[c], term_recv.at[y_hi], target)
-
-    def term_own(c):
-        return pltpu.make_async_copy(leaving.at[pl.ds(c * depth, depth), :], terms.at[y_hi], term_recv.at[y_hi])
-
-    for c in range(2):
-        @pl.when(jnp.logical_not(is_self & (core == c)))
-        def _(c=c):
-            term_copy(c).start()
-
-        @pl.when(is_self & (core == c))
-        def _(c=c):
-            term_own(c).start()
-
-    for n in range(2):
-        pltpu.make_async_copy(terms.at[n], terms.at[n], term_recv.at[n]).wait()
-    total = terms[0].astype(f32) + terms[1].astype(f32)
+        return remote(
+            leaving.at[kind, pl.ds(c * depth, depth), :], terms.at[y_hi, kind],
+            term_send.at[kind, c], term_recv.at[y_hi, kind], target,
+        )
+
+    def term_own(kind, c):
+        return pltpu.make_async_copy(
+            leaving.at[kind, pl.ds(c * depth, depth), :], terms.at[y_hi, kind], term_recv.at[y_hi, kind]
+        )
+
     for kind in range(3):
-        weight_ref[kind] = total[:, kind * LANES : (kind + 1) * LANES]
+        rows = slice(kind * LANES, (kind + 1) * LANES)
+        total = own_total[rows, :]
+        for n in range(last):
+            sum_copy(kind, n).wait_recv()
+            total += from_x[n, rows, :].astype(f32)
+        leaving[kind] = total.T.astype(bf16)
+        for c in range(2):
+            @pl.when(jnp.logical_not(is_self & (core == c)))
+            def _(kind=kind, c=c):
+                term_copy(kind, c).start()
+
+            @pl.when(is_self & (core == c))
+            def _(kind=kind, c=c):
+                term_own(kind, c).start()
+
+    for kind in range(3):
+        for n in range(2):
+            pltpu.make_async_copy(terms.at[n, kind], terms.at[n, kind], term_recv.at[n, kind]).wait()
+        weight_ref[kind] = terms[0, kind].astype(f32) + terms[1, kind].astype(f32)
 
     def await_back(peer, _):
         @pl.when(peer != me)
@@ -383,29 +402,35 @@
     for k in range(HOPS):
         hop(right, me, k).wait_send()
         hop(left, me, k).wait_send()
-    for kind in range(3):
-        for head in range(2):
+    for head in range(2):
+        for index in range(4):
+            turned_block(head, index).wait_send()
+        for kind in range(1, 3):
             turned_copy(kind, head).wait_send()
 
     for n in range(ACROSS):
         sibling_copy(n).wait_send()
-    for n in range(last):
-        sum_copy(n).wait_send()
-    for c in range(2):
-        @pl.when(jnp.logical_not(is_self & (core == c)))
-        def _(c=c):
-            term_copy(c).wait_send()
+    for kind in range(3):
+        for n in range(last):
+            sum_copy(kind, n).wait_send()
+        for c in range(2):
+            @pl.when(jnp.logical_not(is_self & (core == c)))
+            def _(kind=kind, c=c):
+                term_copy(kind, c).wait_send()
 
 
 def copy_out(*refs):
-    count = len(refs) // 2
-    copies = [
-        pltpu.make_async_copy(src, dst, refs[-1].at[n])
-        for n, (src, dst) in enumerate(zip(refs[:count], refs[count:-1]))
-    ]
-    for copy in copies:
+    count = 4
+    sources, targets, held = refs[:count], refs[count : 2 * count], refs[2 * count : 3 * count]
+    arrive, leave = refs[3 * count :]
+    into = [pltpu.make_async_copy(sources[n], held[n], arrive.at[n]) for n in range(count)]
+    out = [pltpu.make_async_copy(held[n], targets[n], leave.at[n]) for n in range(count)]
+    for copy in into:
         copy.start()
-    for copy in copies:
+    for n in range(count):
+        into[n].wait()
+        out[n].start()
+    for copy in out:
         copy.wait()
 
 
@@ -442,8 +467,9 @@
             vmem((ACROSS, 3 * width, columns), bf16),
             vmem((ACROSS - 1, 3 * width, columns), bf16),
             vmem((ACROSS - 1, 3 * width, columns), bf16),
-            vmem((columns, 3 * width), bf16),
-            vmem((2, columns // 2, 3 * width), bf16),
+            vmem((3 * width, columns), f32),
+            vmem((3, columns, width), bf16),
+            vmem((2, 3, columns // 2, width), bf16),
             dma((5,)),
             dma((OWNERS,)),
             dma((OWNERS,)),
@@ -457,12 +483,14 @@
             dma((3, OWNERS)),
             dma((3, 2)),
             dma((3, 2)),
+            dma((2, 4)),
+            dma((2, 4)),
             dma((ACROSS,)),
             dma((ACROSS,)),
-            dma((ACROSS - 1,)),
-            dma((ACROSS - 1,)),
-            dma((2,)),
-            dma((2,)),
+            dma((3, ACROSS - 1)),
+            dma((3, ACROSS - 1)),
+            dma((3, 2)),
+            dma((2, 3)),
         ],
         compiler_params=pltpu.CompilerParams(
             collective_id=0, has_side_effects=True, vmem_limit_bytes=56 * 2**20
@@ -472,9 +500,9 @@
     *back, weight_grad = pl.pallas_call(
         copy_out,
         out_shape=[jax.ShapeDtypeStruct(r.shape, r.dtype) for r in results],
-        in_specs=[whole] * 4,
+        in_specs=[anywhere] * 4,
         out_specs=[anywhere] * 4,
-        scratch_shapes=[dma((4,))],
+        scratch_shapes=[vmem(r.shape, r.dtype) for r in results] + [dma((4,)), dma((4,))],
         name="results",
     )(*results)
     return (*[grad[None] for grad in back], weight_grad)

time: 125 us -> 123 us (0.984)
  no operation moved by 1% of the time
where the time goes in v4:
time: 123 us
  Pallas kernels  121 us (98%)
  between operations  1.29 us (1%)
    pallas_call x1, Pallas kernels, shards(): pl.pallas_call(kernel, out_shape=[jax.ShapeDtypeStruct((rows, features),...  119 us

profile of v4, /device:TPU:2, one launch (start us, length us, event | category | flops | bytes accessed | tf_op | source)
XLA Modules:
  0.0 122.6 jit_solution(16299943810373042508)
XLA Ops:
  1.3 118.9 %attention_and_weights.1 = (bf16[128,2048]{1,0:T(8,128)(2,1)}, bf16[128,2048]{1,0:T(8,128)(2,1)}, bf16[128,2048]{1,0:T(8,128)(2,1)}, f32[3,192,128]{2,1,0:T(8,128)}) custom-call(s32[1]{0:T(128)S(6)} %copy.11.length_ref, bf16[128,2048]{1,0:T(8,128)(2,1)} %bitcast.12, bf16[32,128]{1,0:T(8,128)(2,1)} %bitcast.16, bf16[2048,128]{1,0:T(8,128)(2,1)} %bitcast.13, ...), custom_call_target="tpu_custom_call" | custom-call | tf_op jit(solution)/shard_map/attention_and_weights/pallas_call | solution.py:446
  120.2 2.3 %results.1 = (bf16[128,2048]{1,0:T(8,128)(2,1)}, bf16[128,2048]{1,0:T(8,128)(2,1)}, bf16[128,2048]{1,0:T(8,128)(2,1)}, f32[3,192,128]{2,1,0:T(8,128)}) custom-call(bf16[128,2048]{1,0:T(8,128)(2,1)} %get-tuple-element.12.refs_0_, bf16[128,2048]{1,0:T(8,128)(2,1)} %get-tuple-element.13.refs_1_, bf16[128,2048]{1,0:T(8,128)(2,1)} %get-tuple-element.14.refs_2_, ...), custom_call_target="tpu_custom_call" | custom-call | tf_op jit(solution)/shard_map/results/pallas_call | solution.py:500

commit v5 on v4

--- a/solution.py
+++ b/solution.py
@@ -71,9 +71,6 @@
     own_columns = pl.ds(pl.multiple_of(y_lo * half, LANES), half)
     other_columns = pl.ds(pl.multiple_of((1 - y_lo) * half, LANES), half)
     loads.append(pltpu.make_async_copy(inputs_hbm.at[:, own_columns], gathered.at[me], load_sem.at[3]))
-    for load in loads:
-        load.start()
-
     barrier = pltpu.get_barrier_semaphore()
 
     def greet(d, _):
@@ -91,44 +88,8 @@
             source = {"dp": n * (2 * ACROSS) + x * 2 + y_lo, "seq": y_hi * RING + z}
             pl.semaphore_signal(barrier, inc=1, device_id=source, device_id_type=MESH)
 
-    pl.semaphore_wait(barrier, OWNERS + ACROSS + 1 - jnp.where(is_self, 1, 0))
-
-    swap = remote(inputs_hbm.at[:, other_columns], gathered.at[me], swap_send, swap_recv, partner)
-    swap.start()
-
-    def block_of(kind, place):
-        return jnp.where(kind == 0, y_lo, 1 - y_lo) * RING + (place + RING) % RING
-
-    def hop(to, block, k, src=None):
-        send, recv = (right_send, right_recv) if to is right else (left_send, left_recv)
-        return remote(gathered.at[block] if src is None else src, gathered.at[block], send.at[k], recv.at[k], to)
-
-    def right_block(k):
-        return block_of(k % 2, z - k // 2 - 1)
-
-    def left_block(k):
-        return block_of(jnp.where(k == HOPS - 1, 1, k % 2), z + k // 2 + 1)
-
-    def ring_step(k):
-        hop(right, right_block(k), k).wait_recv()
-
-        @pl.when(k + 2 < HOPS)
-        def _():
-            hop(right, right_block(k), k + 2).start()
-
-        hop(left, left_block(k), k).wait_recv()
-
-        @pl.when(k + 2 < HOPS - 1)
-        def _():
-            hop(left, left_block(k), k + 2).start()
-
-        @pl.when(k == HOPS - 2)
-        def _():
-            hop(left, left_block(k), HOPS - 1).start()
-
-    own_input = inputs_hbm.at[:, own_columns]
-    hop(right, me, 0, own_input).start()
-    hop(left, me, 0, own_input).start()
+    for load in loads:
+        load.start()
 
     heads = factor_ref.shape[0]
     spread = lax.broadcasted_iota(jnp.int32, (heads, heads * HEAD_DIM), 1) // HEAD_DIM
@@ -137,6 +98,45 @@
     live = jnp.where(token < length_ref[0], 1.0, 0.0)
     sent_up[...] = (payload_ref[...].astype(f32) * dot(factor_ref[...], spread, ((0,), (0,))) * live).astype(bf16)
 
+    pl.semaphore_wait(barrier, OWNERS + ACROSS + 1 - jnp.where(is_self, 1, 0))
+
+    swap = remote(inputs_hbm.at[:, other_columns], gathered.at[me], swap_send, swap_recv, partner)
+    swap.start()
+
+    def block_of(kind, place):
+        return jnp.where(kind == 0, y_lo, 1 - y_lo) * RING + (place + RING) % RING
+
+    def hop(to, block, k, src=None):
+        send, recv = (right_send, right_recv) if to is right else (left_send, left_recv)
+        return remote(gathered.at[block] if src is None else src, gathered.at[block], send.at[k], recv.at[k], to)
+
+    def right_block(k):
+        return block_of(k % 2, z - k // 2 - 1)
+
+    def left_block(k):
+        return block_of(jnp.where(k == HOPS - 1, 1, k % 2), z + k // 2 + 1)
+
+    def ring_step(k):
+        hop(right, right_block(k), k).wait_recv()
+
+        @pl.when(k + 2 < HOPS)
+        def _():
+            hop(right, right_block(k), k + 2).start()
+
+        hop(left, left_block(k), k).wait_recv()
+
+        @pl.when(k + 2 < HOPS - 1)
+        def _():
+            hop(left, left_block(k), k + 2).start()
+
+        @pl.when(k == HOPS - 2)
+        def _():
+            hop(left, left_block(k), HOPS - 1).start()
+
+    own_input = inputs_hbm.at[:, own_columns]
+    hop(right, me, 0, own_input).start()
+    hop(left, me, 0, own_input).start()
+
     def up_copy(peer):
         return remote(
             sent_up.at[:, columns_of(peer)], u_ref.at[rows_of(me), :], up_send.at[peer], up_recv.at[me],
@@ -159,6 +159,7 @@
     position = lax.broadcasted_iota(jnp.int32, (positions, LANES), 0)
     lane = lax.broadcasted_iota(jnp.int32, (positions, LANES), 1)
     keys[:, LANES:] = jnp.where((lane == 0) & (position >= length), -1e30, 0.0).astype(bf16)
+    weight_total[...] = jnp.zeros_like(weight_total)
     key_total[...] = jnp.zeros_like(key_total)
     value_total[...] = jnp.zeros_like(value_total)
     for load in loads:
@@ -304,7 +305,6 @@
         at = pl.ds(pl.multiple_of((x + 1 + n) % ACROSS * columns, LANES), columns)
         return weight_total[side, :, at] + product(side, places((RING // 2,)), at)
 
-    weight_total[...] = jnp.zeros_like(weight_total)
     add(y_lo, places((0,)))
     lax.fori_loop(1, 3, add_pair(y_lo), 0)
     ring_step(jnp.int32(HOPS - 3))

time: 123 us -> 123 us (level)
  no operation moved by 1% of the time
where the time goes in v5:
time: 123 us
  Pallas kernels  121 us (98%)
  between operations  1.29 us (1%)
    pallas_call x1, Pallas kernels, shards(): pl.pallas_call(kernel, out_shape=[jax.ShapeDtypeStruct((rows, features),...  119 us

profile of v5, /device:TPU:2, one launch (start us, length us, event | category | flops | bytes accessed | tf_op | source)
XLA Modules:
  0.0 122.5 jit_solution(15402509360862851734)
XLA Ops:
  1.3 118.9 %attention_and_weights.1 = (bf16[128,2048]{1,0:T(8,128)(2,1)}, bf16[128,2048]{1,0:T(8,128)(2,1)}, bf16[128,2048]{1,0:T(8,128)(2,1)}, f32[3,192,128]{2,1,0:T(8,128)}) custom-call(s32[1]{0:T(128)S(6)} %copy.11.length_ref, bf16[128,2048]{1,0:T(8,128)(2,1)} %bitcast.12, bf16[32,128]{1,0:T(8,128)(2,1)} %bitcast.16, bf16[2048,128]{1,0:T(8,128)(2,1)} %bitcast.13, ...), custom_call_target="tpu_custom_call" | custom-call | tf_op jit(solution)/shard_map/attention_and_weights/pallas_call | solution.py:446
  120.2 2.3 %results.1 = (bf16[128,2048]{1,0:T(8,128)(2,1)}, bf16[128,2048]{1,0:T(8,128)(2,1)}, bf16[128,2048]{1,0:T(8,128)(2,1)}, f32[3,192,128]{2,1,0:T(8,128)}) custom-call(bf16[128,2048]{1,0:T(8,128)(2,1)} %get-tuple-element.12.refs_0_, bf16[128,2048]{1,0:T(8,128)(2,1)} %get-tuple-element.13.refs_1_, bf16[128,2048]{1,0:T(8,128)(2,1)} %get-tuple-element.14.refs_2_, ...), custom_call_target="tpu_custom_call" | custom-call | tf_op jit(solution)/shard_map/results/pallas_call | solution.py:500
